TPU v7x, 256 devices: a whole 4x4x8 slice. The times are simulated.
256 devices in a mesh: seq: 64 (over z, x_lo, y), dp: 4 (over x_hi, core).
Axes of the slice: x: 4 (x_hi: 2, x_lo: 2; x = x_hi * 2 + x_lo), y: 4, z: 8, core: 2. Of those that a mesh axis runs over, the one named last changes fastest.
Arguments:
- tokens: bfloat16 [4, 128, 256, 1152], P('dp', 'seq'), may hold values from -500 to 500
- d_out: bfloat16 [4, 128, 256, 1152], P('dp', 'seq'), may hold values from -6 to 6
- modulation: float32 [4, 8, 3, 1152], P('dp'), may hold values from -10 to 10
- w_qkv: bfloat16 [1728, 1152], P('dp'), may hold values from -1 to 1
- w_out: bfloat16 [1152, 576], P('dp'), may hold values from -0.25 to 0.25
Outputs:
- d_tokens: bfloat16 [4, 128, 256, 1152], P('dp', 'seq')
- d_modulation: float32 [4, 8, 3, 1152], P('dp')
- g_qkv: float32 [1728, 1152], P('dp', 'seq')
- g_out: float32 [1152, 576], P('dp', 'seq')
All inputs are finite; a program needn't handle non-finite values.
Results may differ from a plain program's by a relative error of at most 0.0065.
The roundings to bfloat16 on the way count: a program that leaves them out, or rounds other values in their place, can miss the bound.
Values may be sent and summed in bfloat16 or wider, within the bound.
A program may use at most 128 MiB of HBM per device.

v0:
```python
import math

import jax
import jax.numpy as jnp
from jax import lax
from jax.sharding import PartitionSpec as P

HD = 72
HEADS = 8
FRAMES = 16


EPS = 1e-06


def matmul_rows(left, right):
    return lax.dot_general(
        left, right, (((1,), (1,)), ((), ())), preferred_element_type=jnp.float32
    )


def matmul_tokens(left, right):
    return lax.dot_general(
        left, right, (((0,), (0,)), ((), ())), preferred_element_type=jnp.float32
    )


def body(tokens, d_out, modulation, w_qkv, w_out):
    frames_here = tokens.shape[1]
    width = tokens.shape[3]
    clips = modulation.shape[1]
    inv = 1.0 / math.sqrt(HD)
    qkv_full, out_full = (
        lax.all_gather(w_qkv, "dp", axis=0, tiled=True),
        lax.all_gather(w_out, "dp", axis=0, tiled=True),
    )
    own_clip = lax.axis_index("seq") * frames_here // FRAMES
    own_mod = lax.dynamic_index_in_dim(modulation[0], own_clip, 0, keepdims=False)
    shift, scale = (own_mod[0], own_mod[1])
    xf = tokens.astype(jnp.float32)
    center = xf - jnp.mean(xf, -1, keepdims=True)
    var = jnp.mean(center * center, -1, keepdims=True)
    rstd = lax.rsqrt(var + EPS)
    normed = center * rstd
    modulated = (normed * (1.0 + scale) + shift).astype(jnp.bfloat16)
    moved, grad_moved = (
        lax.all_to_all(modulated, "seq", split_axis=2, concat_axis=1, tiled=True),
        lax.all_to_all(d_out, "seq", split_axis=2, concat_axis=1, tiled=True),
    )
    patch_here = moved.shape[2]
    rows = moved.shape[1] * patch_here
    flat_mod = moved.reshape(rows, width)
    qkv = matmul_rows(flat_mod, qkv_full).astype(jnp.bfloat16)
    qkv = qkv.reshape(clips, FRAMES, patch_here, 3, HEADS, HD)
    query, keys, values = (qkv[:, :, :, 0], qkv[:, :, :, 1], qkv[:, :, :, 2])
    scores = jnp.einsum("cfphe,cgphe->cphfg", query, keys, preferred_element_type=jnp.float32) * inv
    probs = jax.nn.softmax(scores, axis=-1)
    probs_b = probs.astype(jnp.bfloat16)
    attended = jnp.einsum("cphfg,cgphe->cfphe", probs_b, values, preferred_element_type=jnp.float32)
    attended = attended.astype(jnp.bfloat16).reshape(rows, HEADS * HD)
    branch = matmul_rows(attended, out_full).reshape(clips, -1, width)
    gates = modulation[0, :, 2, :][:, None, :]
    grad_three = grad_moved.reshape(clips, -1, width).astype(jnp.float32)
    gate_part = jnp.sum(grad_three * branch, 1)
    gate_sum = lax.psum(gate_part, "seq")
    d_branch = (gates * grad_three).astype(jnp.bfloat16).reshape(rows, width)
    g_out = matmul_tokens(d_branch, attended)
    d_att = jnp.dot(d_branch, out_full, preferred_element_type=jnp.float32).astype(jnp.bfloat16)
    d_att = d_att.reshape(clips, FRAMES, patch_here, HEADS, HD)
    d_probs = jnp.einsum("cfphe,cgphe->cphfg", d_att, values, preferred_element_type=jnp.float32)
    d_values = jnp.einsum("cphfg,cfphe->cgphe", probs_b, d_att, preferred_element_type=jnp.float32)
    d_scores = (probs * (d_probs - jnp.sum(probs * d_probs, -1, keepdims=True)) * inv).astype(
        jnp.bfloat16
    )
    d_query = jnp.einsum("cphfg,cgphe->cfphe", d_scores, keys, preferred_element_type=jnp.float32)
    d_keys = jnp.einsum("cphfg,cfphe->cgphe", d_scores, query, preferred_element_type=jnp.float32)
    d_qkv = (
        jnp.stack([d_query, d_keys, d_values], 3).astype(jnp.bfloat16).reshape(rows, 3 * HEADS * HD)
    )
    g_qkv = matmul_tokens(d_qkv, flat_mod)
    d_mod_in = jnp.dot(d_qkv, qkv_full, preferred_element_type=jnp.float32).astype(jnp.bfloat16)
    returned = lax.all_to_all(
        d_mod_in.reshape(moved.shape), "seq", split_axis=1, concat_axis=2, tiled=True
    )
    d_back = returned.astype(jnp.float32)
    shift_part = jnp.sum(d_back, (0, 1, 2))
    scale_part = jnp.sum(d_back * normed, (0, 1, 2))
    d_normed = d_back * (1.0 + scale)
    mean_one = jnp.mean(d_normed, -1, keepdims=True)
    mean_two = jnp.mean(d_normed * normed, -1, keepdims=True)
    d_tokens = (
        d_out.astype(jnp.float32) + rstd * (d_normed - mean_one - normed * mean_two)
    ).astype(jnp.bfloat16)
    marker = (jnp.arange(clips) == own_clip).astype(jnp.float32)[:, None, None]
    local_part = jnp.stack([shift_part, scale_part], 0)[None] * marker
    local_sum = lax.psum(local_part, "seq")
    d_modulation = jnp.concatenate([local_sum, gate_sum[:, None, :]], 1)[None]
    g_qkv, g_out = (
        lax.psum_scatter(g_qkv, "seq", scatter_dimension=1, tiled=True),
        lax.psum_scatter(g_out, "seq", scatter_dimension=1, tiled=True),
    )
    g_qkv, g_out = (
        lax.psum_scatter(g_qkv, "dp", scatter_dimension=0, tiled=True),
        lax.psum_scatter(g_out, "dp", scatter_dimension=0, tiled=True),
    )
    return (d_tokens, d_modulation, g_qkv, g_out)


def solution(mesh):
    in_specs = (
        P("dp", "seq", None, None),
        P("dp", "seq", None, None),
        P("dp", None, None, None),
        P("dp", None),
        P("dp", None),
    )
    out_specs = (
        P("dp", "seq", None, None),
        P("dp", None, None, None),
        P("dp", "seq"),
        P("dp", "seq"),
    )
    return jax.shard_map(body, mesh=mesh, in_specs=in_specs, out_specs=out_specs, check_vma=False)
```

profile of v0, /device:TPU:1, one launch (start us, length us, event | category | flops | bytes accessed | tf_op | source)
XLA Modules:
  0.0 1180.6 jit_solution(5214333125747187485)
XLA Ops:
  10.9 13.6 %all-to-all-start.1 = ((bf16[1,2,256,1152]{3,1,0,2:T(2,128)(2,1)}), bf16[1,2,256,1152]{3,1,0,2:T(2,128)(2,1)S(1)}, u32[]{:S(2)}, u32[]{:S(2)}) async-start(bf16[1,2,256,1152]{3,1,0,2:T(2,128)(2,1)} %copy.33), calls=%async_computation.1 | async-start | bytes 2359296 | tf_op jit(solution)/shard_map/all_to_all | solution.py:48
  29.4 3.3 add_convert_fusion.1
  32.7 20.5 %all-to-all-done.1 = bf16[1,2,256,1152]{3,1,0,2:T(2,128)(2,1)S(1)} async-done(((bf16[1,2,256,1152]{3,1,0,2:T(2,128)(2,1)}), bf16[1,2,256,1152]{3,1,0,2:T(2,128)(2,1)S(1)}, u32[]{:S(2)}, u32[]{:S(2)}) %all-to-all-start.1) | async-done | bytes 1179680 | tf_op jit(solution)/shard_map/all_to_all | solution.py:48
  53.2 8.5 all-to-all-start
  74.9 14.1 %all-to-all-done = bf16[1,2,256,1152]{3,1,0,2:T(2,128)(2,1)} async-done(((bf16[1,2,256,1152]{3,1,0,2:T(2,128)(2,1)}), bf16[1,2,256,1152]{3,1,0,2:T(2,128)(2,1)}, u32[]{:S(2)}, u32[]{:S(2)}) %all-to-all-start) | async-done | bytes 1179680 | tf_op jit(solution)/shard_map/all_to_all | solution.py:47
  91.1 9.8 all-gather.3.cloned.1.call-done
  100.9 5.9 convolution_convert_fusion
  109.6 4.5 reshape.164
  114.1 4.0 fusion.33
  118.1 4.7 fusion.35
  126.6 6.0 convolution_bitcast_fusion.1
  132.6 4.8 convolution_bitcast_fusion.2
  142.4 4.9 convert_element_type.145
  147.4 7.0 fusion.36
  154.3 3.6 convolution_convert_fusion.1
  157.9 3.2 reshape.166
  161.1 10.1 all-to-all-start.2
  171.3 191.5 %fusion = f32[1728,24]{0,1:T(8,128)} fusion(f32[1728,1152]{0,1:T(8,128)} %fusion.36), kind=kCustom, calls=%all-reduce-scatter | all-reduce-scatter fusion | flops 2654209 | bytes 8129536
  370.3 5.4 collective-permute-start.14
  382.9 8.4 collective-permute-start.9
  391.4 4.3 collective-permute-start.8
  397.7 3.5 collective-permute-start.6
  411.9 3.2 collective-permute-start.3
  417.9 4.3 collective-permute-start.1
  424.1 4.0 fusion.37
  428.1 28.8 %concatenate.4 = f32[1728,402]{0,1:T(8,128)} concatenate(f32[1728,18]{0,1:T(8,128)} %collective-permute-done.15, f32[1728,24]{0,1:T(8,128)} %copy-done.16, f32[1728,24]{0,1:T(8,128)} %copy-done.17, f32[1728,24]{0,1:T(8,128)} %copy-done.18, f32[1728,24]{0,1:T(8,128)} %copy-done.19, f32[1728,24]{0,1:T(8,128)} %copy-done.20, f32[1728,24]{0,1:T(8,128)} %collective-permute-done.9, ...), dimensions={1} | concatenate | bytes 5557248
  463.8 5.0 multiply_reduce_fusion
  474.7 3.4 fusion.12
  478.2 251.6 %psum.15 = f32[8,1,1152]{2,0,1:T(8,128)} all-reduce(f32[8,1,1152]{2,0,1:T(8,128)} %bitcast.106), channel_id=1, replica_groups=mesh['seq'=64,'dp'=4] {'seq'}, use_global_device_ids=true, to_apply=%region_11.12 | all-reduce | flops 9216 | bytes 73728 | tf_op jit(solution)/shard_map/psum | solution.py:65
  737.2 5.3 add_convert_fusion
  743.7 351.9 %all-reduce.6.cloned.1.call-done = (f32[8,2,1152]{2,0,1:T(8,128)}, f32[1152,576]{0,1:T(8,128)}) async-done(((f32[8,2,1152]{2,0,1:T(8,128)}, f32[1152,576]{0,1:T(8,128)}), (f32[8,2,1152]{2,0,1:T(8,128)}, f32[1152,576]{0,1:T(8,128)})) %all-reduce.6.cloned.1.call-update) | async-done | bytes 2727952 | tf_op jit(solution)/shard_map/psum | solution.py:96
  1099.2 72.9 %reduce-scatter.11.cloned.1.call-done = f32[288,9]{1,0:T(8,128)} async-done(((f32[1152,9]{1,0:T(8,128)}), f32[288,9]{1,0:T(8,128)}) %reduce-scatter.11.cloned.1.call-update) | async-done | bytes 10384
  (143 shorter events, 92.7 us)
Async XLA Ops:
  7.2 62.7 %all-gather.5.cloned.1.call-start = ((), (), s32[]{:S(2)}) async-start(), calls=%async_computation.6 | async-start | bytes 1843200 | tf_op jit(solution)/shard_map/all_gather | solution.py:35
  7.9 93.0 %all-gather.3.cloned.1.call-start = ((), (), s32[]{:S(2)}) async-start(), calls=%async_computation.5 | async-start | bytes 4976640 | tf_op jit(solution)/shard_map/all_gather | solution.py:34
  8.7 16.7 %copy-start = (bf16[1,2,256,1152]{3,2,1,0:T(8,128)(2,1)S(1)}, bf16[1,2,256,1152]{3,2,1,0:T(8,128)(2,1)}, u32[]{:S(2)}) copy-start(bf16[1,2,256,1152]{3,2,1,0:T(8,128)(2,1)} %param.5) | copy-start | bytes 3538948
  10.9 42.3 %all-to-all-start.1 = ((bf16[1,2,256,1152]{3,1,0,2:T(2,128)(2,1)}), bf16[1,2,256,1152]{3,1,0,2:T(2,128)(2,1)S(1)}, u32[]{:S(2)}, u32[]{:S(2)}) async-start(bf16[1,2,256,1152]{3,1,0,2:T(2,128)(2,1)} %copy.33), calls=%async_computation.1 | async-start | bytes 2359296 | tf_op jit(solution)/shard_map/all_to_all | solution.py:48
  53.2 35.8 %all-to-all-start = ((bf16[1,2,256,1152]{3,1,0,2:T(2,128)(2,1)}), bf16[1,2,256,1152]{3,1,0,2:T(2,128)(2,1)}, u32[]{:S(2)}, u32[]{:S(2)}) async-start(bf16[1,2,256,1152]{3,1,0,2:T(2,128)(2,1)} %add_convert_fusion.1), calls=%async_computation | async-start | bytes 2359296 | tf_op jit(solution)/shard_map/all_to_all | solution.py:47
  161.1 299.6 %all-to-all-start.2 = ((bf16[1,128,4,1152]{3,2,0,1:T(4,128)(2,1)}), bf16[1,128,4,1152]{3,2,0,1:T(4,128)(2,1)}, u32[]{:S(2)}, u32[]{:S(2)}) async-start(bf16[1,128,4,1152]{3,2,0,1:T(4,128)(2,1)} %bitcast.15), calls=%async_computation.2 | async-start | bytes 2359296 | tf_op jit(solution)/shard_map/all_to_all | solution.py:82
  171.2 195.1 %copy-start.22 = (u32[256]{0:T(256)S(1)}, u32[256]{0:T(256)}, u32[]{:S(2)}) copy-start(u32[256]{0:T(256)} %constant.52) | copy-start | bytes 3076
  171.2 558.5 %reduce-scatter.9.cloned.1.call-start = ((), (), s32[]{:S(2)}) async-start(), calls=%async_computation.7 | async-start | bytes 1105920
  364.4 15.3 %collective-permute-start.15 = (f32[1728,18]{0,1:T(8,128)}, f32[1728,18]{0,1:T(8,128)}, u32[]{:S(2)}, u32[]{:S(2)}) collective-permute-start(f32[1728,18]{0,1:T(8,128)} %slice.29), channel_id=1, source_target_pairs={{0,64},{4,68},{8,72},{12,76},{16,80},{20,84},{24,88},{28,92},{32,9... | collective-permute-start | bytes 373256
  370.2 34.1 %copy-start.9 = (bf16[8,16,4,1,8,72]{5,4,3,2,1,0:T(8,128)(2,1)S(1)}, bf16[8,16,4,1,8,72]{5,4,3,2,1,0:T(8,128)(2,1)}, u32[]{:S(2)}) copy-start(bf16[8,16,4,1,8,72]{5,4,3,2,1,0:T(8,128)(2,1)} %copy-done.8) | copy-start | bytes 1769476
  370.2 34.1 %copy-start.25 = (f32[8,4,8,16,16]{3,4,2,1,0:T(8,128)S(1)}, f32[8,4,8,16,16]{3,4,2,1,0:T(8,128)}, u32[]{:S(2)}) copy-start(f32[8,4,8,16,16]{3,4,2,1,0:T(8,128)} %get-tuple-element.20) | copy-start | bytes 786436
  370.3 34.1 %copy-start.27 = (f32[8,4,8,16]{3,2,1,0:T(8,128)S(1)}, f32[8,4,8,16]{3,2,1,0:T(8,128)}, u32[]{:S(2)}) copy-start(f32[8,4,8,16]{3,2,1,0:T(8,128)} %copy-done.26) | copy-start | bytes 49156
  370.3 12.7 %collective-permute-start.14 = (f32[1728,24]{0,1:T(8,128)}, f32[1728,24]{0,1:T(8,128)S(1)}, u32[]{:S(2)}, u32[]{:S(2)}) collective-permute-start(f32[1728,24]{0,1:T(8,128)} %fusion), channel_id=1, source_target_pairs={{0,60},{4,64},{8,68},{12,72},{16,76},{20,80},{24,84},{28,88},{32,9... | collective-permute-start | bytes 497672
  375.7 15.7 %collective-permute-start.13 = (f32[1728,24]{0,1:T(8,128)}, f32[1728,24]{0,1:T(8,128)S(1)}, u32[]{:S(2)}, u32[]{:S(2)}) collective-permute-start(f32[1728,24]{0,1:T(8,128)} %fusion), channel_id=1, source_target_pairs={{0,56},{4,60},{8,64},{12,68},{16,72},{20,76},{24,80},{28,84},{32,8... | collective-permute-start | bytes 497672
  377.0 18.7 %collective-permute-start.12 = (f32[1728,24]{0,1:T(8,128)}, f32[1728,24]{0,1:T(8,128)S(1)}, u32[]{:S(2)}, u32[]{:S(2)}) collective-permute-start(f32[1728,24]{0,1:T(8,128)} %fusion), channel_id=1, source_target_pairs={{0,52},{4,56},{8,60},{12,64},{16,68},{20,72},{24,76},{28,80},{32,8... | collective-permute-start | bytes 497672
  378.3 19.4 %collective-permute-start.11 = (f32[1728,24]{0,1:T(8,128)}, f32[1728,24]{0,1:T(8,128)S(1)}, u32[]{:S(2)}, u32[]{:S(2)}) collective-permute-start(f32[1728,24]{0,1:T(8,128)} %fusion), channel_id=1, source_target_pairs={{0,48},{4,52},{8,56},{12,60},{16,64},{20,68},{24,72},{28,76},{32,8... | collective-permute-start | bytes 497672
  379.6 21.5 %collective-permute-start.10 = (f32[1728,24]{0,1:T(8,128)}, f32[1728,24]{0,1:T(8,128)S(1)}, u32[]{:S(2)}, u32[]{:S(2)}) collective-permute-start(f32[1728,24]{0,1:T(8,128)} %fusion), channel_id=1, source_target_pairs={{0,44},{4,48},{8,52},{12,56},{16,60},{20,64},{24,68},{28,72},{32,7... | collective-permute-start | bytes 497672
  382.9 18.2 %copy-start.16 = (f32[1728,24]{0,1:T(8,128)}, f32[1728,24]{0,1:T(8,128)S(1)}, u32[]{:S(2)}) copy-start(f32[1728,24]{0,1:T(8,128)S(1)} %collective-permute-done.14) | copy-start | bytes 497668
  382.9 26.1 %collective-permute-start.9 = (f32[1728,24]{0,1:T(8,128)}, f32[1728,24]{0,1:T(8,128)}, u32[]{:S(2)}, u32[]{:S(2)}) collective-permute-start(f32[1728,24]{0,1:T(8,128)} %fusion), channel_id=1, source_target_pairs={{0,40},{4,44},{8,48},{12,52},{16,56},{20,60},{24,64},{28,68},{32,7... | collective-permute-start | bytes 497672
  391.4 20.5 %collective-permute-start.8 = (f32[1728,24]{0,1:T(8,128)}, f32[1728,24]{0,1:T(8,128)}, u32[]{:S(2)}, u32[]{:S(2)}) collective-permute-start(f32[1728,24]{0,1:T(8,128)} %fusion), channel_id=1, source_target_pairs={{0,36},{4,40},{8,44},{12,48},{16,52},{20,56},{24,60},{28,64},{32,6... | collective-permute-start | bytes 497672
  395.7 19.3 %collective-permute-start.7 = (f32[1728,24]{0,1:T(8,128)}, f32[1728,24]{0,1:T(8,128)}, u32[]{:S(2)}, u32[]{:S(2)}) collective-permute-start(f32[1728,24]{0,1:T(8,128)} %fusion), channel_id=1, source_target_pairs={{0,32},{4,36},{8,40},{12,44},{16,48},{20,52},{24,56},{28,60},{32,6... | collective-permute-start | bytes 497672
  397.7 20.2 %collective-permute-start.6 = (f32[1728,24]{0,1:T(8,128)}, f32[1728,24]{0,1:T(8,128)}, u32[]{:S(2)}, u32[]{:S(2)}) collective-permute-start(f32[1728,24]{0,1:T(8,128)} %fusion), channel_id=1, source_target_pairs={{0,28},{4,32},{8,36},{12,40},{16,44},{20,48},{24,52},{28,56},{32,6... | collective-permute-start | bytes 497672
  401.8 20.3 %collective-permute-start.5 = (f32[1728,24]{0,1:T(8,128)}, f32[1728,24]{0,1:T(8,128)}, u32[]{:S(2)}, u32[]{:S(2)}) collective-permute-start(f32[1728,24]{0,1:T(8,128)} %fusion), channel_id=1, source_target_pairs={{0,24},{4,28},{8,32},{12,36},{16,40},{20,44},{24,48},{28,52},{32,5... | collective-permute-start | bytes 497672
  409.0 19.0 %collective-permute-start.4 = (f32[1728,24]{0,1:T(8,128)}, f32[1728,24]{0,1:T(8,128)}, u32[]{:S(2)}, u32[]{:S(2)}) collective-permute-start(f32[1728,24]{0,1:T(8,128)} %fusion), channel_id=1, source_target_pairs={{0,20},{4,24},{8,28},{12,32},{16,36},{20,40},{24,44},{28,48},{32,5... | collective-permute-start | bytes 497672
  411.9 16.2 %collective-permute-start.3 = (f32[1728,24]{0,1:T(8,128)}, f32[1728,24]{0,1:T(8,128)}, u32[]{:S(2)}, u32[]{:S(2)}) collective-permute-start(f32[1728,24]{0,1:T(8,128)} %fusion), channel_id=1, source_target_pairs={{0,16},{4,20},{8,24},{12,28},{16,32},{20,36},{24,40},{28,44},{32,4... | collective-permute-start | bytes 497672
  415.1 13.0 %collective-permute-start.2 = (f32[1728,24]{0,1:T(8,128)}, f32[1728,24]{0,1:T(8,128)}, u32[]{:S(2)}, u32[]{:S(2)}) collective-permute-start(f32[1728,24]{0,1:T(8,128)} %fusion), channel_id=1, source_target_pairs={{0,12},{4,16},{8,20},{12,24},{16,28},{20,32},{24,36},{28,40},{32,4... | collective-permute-start | bytes 497672
  417.9 10.2 collective-permute-start.1
  422.1 5.9 collective-permute-start
  460.7 634.9 %all-reduce.6.cloned.1.call-start = ((), (), s32[]{:S(2)}) async-start(), calls=%async_computation.9 | async-start | bytes 5455872 | tf_op jit(solution)/shard_map/psum | solution.py:96
  471.3 700.7 %reduce-scatter.11.cloned.1.call-start = ((), (), s32[]{:S(2)}) async-start(), calls=%async_computation.8 | async-start | bytes 737280
  478.2 259.1 %copy-start.4 = (f32[1,2,64,4,1152]{4,1,3,2,0:T(2,128)S(1)}, f32[1,2,64,4,1152]{4,1,3,2,0:T(2,128)}, u32[]{:S(2)}) copy-start(f32[1,2,64,4,1152]{4,1,3,2,0:T(2,128)} %copy-done.3) | copy-start | bytes 7077892
  742.6 355.0 %copy-start.21 = (f32[8,1,1152]{2,0,1:T(8,128)S(1)}, f32[8,1,1152]{2,0,1:T(8,128)}, u32[]{:S(2)}) copy-start(f32[8,1,1152]{2,0,1:T(8,128)} %psum.15) | copy-start | bytes 110596
  (20 other events, 91.1 us)
Sparse Core Ops, SparseCore 0:
  9.8 37.3 all-gather.4
  49.0 51.9 all-gather.2
  460.8 69.8 reduce-scatter.8
  534.0 561.5 all-reduce.5
  1098.2 73.7 reduce-scatter.10
where the time goes:
time: 1190 us; the launch traced here: 1180 us
  waiting for transfers between devices  471 us (40%)
  blocking collectives  443 us (37%)
  local copies, waits for them, and re-layouts  89.1 us (7%)
  starting transfers between devices  80.7 us (7%)
  matrix products  46.4 us (4%)
  other arithmetic  34.7 us (3%)
  between operations  16 us (1%)
    psum x1, waiting for transfers between devices, body(): local_sum = lax.psum(local_part, 'seq')  352 us
    psum x1, blocking collectives, body(): gate_sum = lax.psum(gate_part, 'seq')  252 us
    unnamed x1, blocking collectives  191 us
    unnamed x23, waiting for transfers between devices  74.3 us
    unnamed x18, starting transfers between devices  48.4 us
    unnamed x67, local copies, waits for them, and re-layouts  45 us
  transfers between devices with their start and end apart: 24, of which 5 were waited for; matrix products, arithmetic and copies ran while one was open for 25% of the time, Pallas kernels for 0%

commit v1 on v0

v1 whole, which is shorter than its diff:
```python
import functools
import math

import jax
import jax.numpy as jnp
from jax import lax
from jax.experimental import pallas as pl
from jax.experimental.pallas import tpu as pltpu
from jax.sharding import PartitionSpec as P

MESH = pl.DeviceIdType.MESH
F32 = jnp.float32
BF16 = jnp.bfloat16

WIDTH = 1152
HEADS = 8
HD = 72
FRAMES = 16
CLIP_DEVICES = 8
CHUNKS = 4
CHUNK = 128
ROWS = 512
SHARD_Q = 432
SHARD_O = 288
HALF_Q = 896
HALF_O = 640
START_O = 512
SLOT_E = 80
EPS = 1e-06
VMEM_BYTES = 56 * 1024 * 1024
NEG = -1e30

PIECES = ((0, 0, 512), (0, 512, 384), (1, 0, 256), (1, 256, 384))
FIRST_PIECES = ((0, 2), (1, 3))
BLOCK_Q = 144
BLOCK_O = SLOT_E
OFFSETS = (4, 3, 5, 2, 6, 1, 7, 0)
STEPS = 4


def dot(left, right, contract):
    return lax.dot_general(
        left, right, ((contract[:1], contract[1:]), ((), ())), preferred_element_type=F32
    )


def place():
    seq, dp = lax.axis_index("seq"), lax.axis_index("dp")
    clip, spot = lax.div(seq, 8), lax.rem(seq, 8)
    half, core = lax.div(dp, 2), lax.rem(dp, 2)
    return seq, dp, clip, spot, half, core


def column(part, head):
    block = part * HEADS + head
    return block * HD if block < 12 else HALF_Q + (block - 12) * HD


def normalise(x):
    center = x - jnp.mean(x, -1, keepdims=True)
    var = jnp.mean(center * center, -1, keepdims=True)
    rstd = lax.rsqrt(var + EPS)
    return center * rstd, rstd


def signal_all(barrier, devices):
    for device in devices:
        pl.semaphore_signal(barrier, inc=1, device_id=device, device_id_type=MESH)


def wait_bytes(ref, sem):
    pltpu.make_async_copy(ref, ref, sem).wait()


def spread_kernel(
    tok, dout, mod, wq, wo, m_all, d_all, wq_all, wo_all,
    m_send, d_send, a_send, a_recv, w_send, w_recv, here,
):
    seq, dp, clip, spot, half, core = place()
    twin = {"seq": seq, "dp": half * 2 + 1 - core}
    across = {
        "seq": clip * 8 + (1 - lax.div(spot, 4)) * 4 + lax.rem(spot, 4),
        "dp": (1 - half) * 2 + core,
    }

    def peer(d):
        return {"seq": clip * 8 + lax.rem(spot + d, 8), "dp": dp}

    barrier = pltpu.get_barrier_semaphore()
    signal_all(barrier, [peer(d) for d in range(1, 8)] + [twin, across])
    pl.semaphore_wait(barrier, 9)

    def rows(h, c):
        return (
            wq_all.at[pl.ds(pl.multiple_of(h * HALF_Q + c * SHARD_Q, 16), SHARD_Q)],
            wo_all.at[pl.ds(pl.multiple_of((h * 2 + c) * SHARD_O, 16), SHARD_O)],
        )

    def push(src, dst, at, device):
        copies = [
            pltpu.make_async_remote_copy(
                src_ref=src[i], dst_ref=dst[i], send_sem=w_send.at[at + i],
                recv_sem=w_recv.at[at + i], device_id=device, device_id_type=MESH,
            )
            for i in range(2)
        ]
        for copy in copies:
            copy.start()
        return copies

    own = rows(half, core)
    sent = push((wq, wo), own, 2, across)
    sent += push((wq, wo), own, 0, twin)
    locals_ = [pltpu.make_async_copy(src, own[i], here.at[i]) for i, src in enumerate((wq, wo))]
    for copy in locals_:
        copy.start()
    zeros = jnp.zeros((HALF_Q - 2 * SHARD_Q, WIDTH), BF16)
    wq_all[2 * SHARD_Q:HALF_Q, :] = zeros
    wq_all[HALF_Q + 2 * SHARD_Q:, :] = zeros

    own_mod = mod[0, pl.ds(clip, 1)].reshape(3, WIDTH)
    shift, scale = own_mod[0:1], 1.0 + own_mod[1:2]

    def arranged(x):
        return jnp.concatenate(
            [x[f, 8 * g:8 * g + 8] for g in range(CHUNKS) for f in range(2)], 0
        ).astype(BF16).reshape(CHUNKS, 16, WIDTH)

    def blocks(d):
        first = pl.multiple_of(lax.rem(spot + d, 8) * 32, 32)
        x = tok[0, :, pl.ds(first, 32), :].astype(F32)
        g = dout[0, :, pl.ds(first, 32), :].astype(F32)
        normed, _ = normalise(x)
        return arranged(normed * scale + shift), arranged(g)

    mine = pl.ds(pl.multiple_of(spot * 16, 16), 16)

    def copies(d):
        return [
            pltpu.make_async_remote_copy(
                src_ref=src.at[d], dst_ref=dst.at[:, mine, :], send_sem=a_send.at[i, d],
                recv_sem=a_recv.at[i, d], device_id=peer(d), device_id_type=MESH,
            )
            for i, (src, dst) in enumerate(((m_send, m_all), (d_send, d_all)))
        ]

    @pl.loop(1, 8)
    def _(d):
        m_send[d], d_send[d] = blocks(d)
        for copy in copies(d):
            copy.start()

    m_all[:, mine, :], d_all[:, mine, :] = blocks(0)
    other = rows(1 - half, core)
    for i in range(2):
        wait_bytes(other[i], w_recv.at[2 + i])
    sent += push(other, other, 4, twin)
    last = rows(1 - half, 1 - core)
    for i, ref in enumerate(rows(half, 1 - core)):
        wait_bytes(ref, w_recv.at[i])
    for d in range(1, 8):
        for copy in copies(d):
            copy.wait_recv()
    for i, ref in enumerate(last):
        wait_bytes(ref, w_recv.at[4 + i])
    for d in range(1, 8):
        for copy in copies(d):
            copy.wait_send()
    for copy in sent:
        copy.wait_send()
    for copy in locals_:
        copy.wait()


def middle_kernel(
    m_all, d_all, wq_all, wo_all, mod, d_in, gq, go, gate_part,
    qkv, datt, att, att_slots, dbranch, dqkv, turned,
):
    _, _, clip, _, _, _ = place()
    gate = mod[0, pl.ds(clip, 1)].reshape(3, WIDTH)[2:3]
    inv = 1.0 / math.sqrt(HD)

    m = m_all[...].reshape(ROWS, WIDTH)

    @pl.loop(0, 7)
    def _(n):
        at = pl.ds(pl.multiple_of(n * 256, 256), 256)
        qkv[:, at] = dot(m, wq_all[at, :], (1, 1)).astype(BF16)

    @pl.loop(0, CHUNKS)
    def _(c):
        at = pl.ds(pl.multiple_of(c * CHUNK, CHUNK), CHUNK)
        dbranch[at, :] = (gate * d_all[c].astype(F32)).astype(BF16)

    datt[...] = dot(dbranch[...], wo_all[...], (1, 0)).astype(BF16)

    for ref, start in ((dqkv, 2 * SHARD_Q), (dqkv, HALF_Q + 2 * SHARD_Q)):
        ref[:, start:start + 32] = jnp.zeros((ROWS, 32), BF16)
    att_slots[...] = jnp.zeros_like(att_slots)

    same = lax.rem(lax.broadcasted_iota(jnp.int32, (CHUNK, CHUNK), 0), 8) == lax.rem(
        lax.broadcasted_iota(jnp.int32, (CHUNK, CHUNK), 1), 8
    )

    @pl.loop(0, CHUNKS)
    def _(c):
        at = pl.ds(pl.multiple_of(c * CHUNK, CHUNK), CHUNK)
        for h in range(HEADS):
            cq, ck, cv = (column(part, h) for part in range(3))
            q, k, v = (qkv[at, col:col + HD] for col in (cq, ck, cv))
            da = datt[at, h * HD:h * HD + HD]
            scores = jnp.where(same, dot(q, k, (1, 1)) * inv, NEG)
            e = jnp.exp(scores - jnp.max(scores, -1, keepdims=True))
            probs = e / jnp.sum(e, -1, keepdims=True)
            probs_b = probs.astype(BF16)
            attended = dot(probs_b, v, (1, 0)).astype(BF16)
            att[at, h * HD:h * HD + HD] = attended
            att_slots[at, h * SLOT_E:h * SLOT_E + HD] = attended
            d_probs = dot(da, v, (1, 1))
            spread = jnp.sum(probs * d_probs, -1, keepdims=True)
            d_scores = (probs * (d_probs - spread) * inv).astype(BF16)
            dqkv[at, cq:cq + HD] = dot(d_scores, k, (1, 0)).astype(BF16)
            dqkv[at, ck:ck + HD] = dot(d_scores, q, (0, 0)).astype(BF16)
            dqkv[at, cv:cv + HD] = dot(probs_b, da, (0, 0)).astype(BF16)

    for n in range(3):
        at = slice(n * 384, n * 384 + 384)
        part = dot(dqkv[...], wq_all[:, at], (1, 0)).astype(BF16)
        d_in[:, :, at] = part.reshape(CHUNKS, CHUNK, 384)

    turned[...] = m.T
    for h in range(2):
        @pl.loop(0, 7)
        def _(n):
            at = pl.ds(pl.multiple_of(n * 128, 128), 128)
            src = pl.ds(pl.multiple_of(h * HALF_Q + n * 128, 128), 128)
            gq[h, :, at] = dot(turned[...], dqkv[:, src], (1, 0)).astype(BF16)

    slots = att_slots[...].T
    for h in range(2):
        go[h] = dot(slots, dbranch[:, h * START_O:h * START_O + HALF_O], (1, 0)).astype(BF16)

    for n in range(3):
        at = slice(n * 384, n * 384 + 384)
        branch = dot(att[...], wo_all[at, :], (1, 1))
        grads = d_all[:, :, at].reshape(ROWS, 384).astype(F32)
        gate_part[:, at] = jnp.sum(branch * grads, 0, keepdims=True)


def finish_kernel(
    d_in, gq, go, gate_part, tok, dout, mod, d_tok, d_mod, oq, oo,
    back, xq, xo, sq, so, rq, ro, stage, final, part, parts,
    b_send, b_recv, x_send, x_recv, c_send, c_recv, p_send, p_recv,
    z_send, z_recv, f_send, f_recv,
):
    seq, dp, clip, spot, half, core = place()
    twin = {"seq": seq, "dp": half * 2 + 1 - core}

    def peer(d):
        return {"seq": clip * 8 + lax.rem(spot + d, 8), "dp": dp}

    def along(d):
        return {"seq": lax.rem(clip + d, 8) * 8 + spot, "dp": dp}

    def owner(d, low):
        return {"seq": clip * 8 + lax.rem(spot + d, 8), "dp": core * 2 + low}

    def source(d, h):
        return {"seq": clip * 8 + lax.rem(spot + 8 - d, 8), "dp": h * 2 + half}

    barrier = pltpu.get_barrier_semaphore()
    signal_all(barrier, [twin] + [peer(d) for d in range(1, 8)] + [along(d) for d in range(1, 8)])
    signal_all(barrier, [source(d, h) for d in range(1, 8) for h in range(2)])
    for h in range(2):
        @pl.when(jnp.logical_or(half != core, h != half))
        def _():
            signal_all(barrier, [source(0, h)])
    pl.semaphore_wait(barrier, jnp.where(half == core, 30, 31))

    def back_copy(d):
        to = pl.ds(pl.multiple_of(lax.rem(spot + d, 8) * 16, 16), 16)
        return pltpu.make_async_remote_copy(
            src_ref=d_in.at[:, to, :], dst_ref=back.at[d], send_sem=b_send.at[d],
            recv_sem=b_recv.at[d], device_id=peer(d), device_id_type=MESH,
        )

    for d in range(1, 8):
        back_copy(d).start()

    def block(ref, z):
        size = BLOCK_Q if ref is xq or ref is gq else BLOCK_O
        return pl.ds(pl.multiple_of(z * size, 16), size)

    def pair_copies(i):
        z = lax.rem(clip + OFFSETS[i], 8)
        return [
            pltpu.make_async_remote_copy(
                src_ref=src.at[1 - core, block(dst, z), :], dst_ref=dst.at[block(dst, z), :],
                send_sem=x_send.at[i, n], recv_sem=x_recv.at[i, n],
                device_id=twin, device_id_type=MESH,
            )
            for n, (src, dst) in enumerate(((gq, xq), (go, xo)))
        ]

    for i in range(8):
        for copy in pair_copies(i):
            copy.start()

    def own(which, z, first, lanes):
        src, dst = (gq, xq) if which == 0 else (go, xo)
        at = block(dst, z)
        return src[core, at, first:first + lanes].astype(F32) + dst[at, first:first + lanes].astype(F32)

    def pieces(k, way):
        return FIRST_PIECES[way] if k == 0 else range(len(PIECES))

    def chain_copy(way, k, n):
        which, first, lanes = PIECES[n]
        src, dst = (sq, rq) if which == 0 else (so, ro)
        return pltpu.make_async_remote_copy(
            src_ref=src.at[way, k, :, first:first + lanes],
            dst_ref=dst.at[way, k, :, first:first + lanes],
            send_sem=c_send.at[way, k, n], recv_sem=c_recv.at[way, k, n],
            device_id=along(1 if way == 0 else 7), device_id_type=MESH,
        )

    def arrived(way, k, n):
        which, first, lanes = PIECES[n]
        chain_copy(way, k, n).wait_recv()
        return (rq, ro)[which][way, k, :, first:first + lanes].astype(F32)

    def chain_step(k):
        for way in range(2):
            for copy in pair_copies(0 if k == 0 else 2 * k - 1 + way) if not (k == 0 and way) else []:
                copy.wait_recv()
        for n in range(len(PIECES)):
            for way in range(2):
                if n not in pieces(k, way):
                    continue
                which, first, lanes = PIECES[n]
                z = lax.rem(clip + (4 - k if way == 0 else 4 + k), 8)
                total = own(which, z, first, lanes)
                if k and n in pieces(k - 1, way):
                    total = total + arrived(way, k - 1, n)
                (sq, so)[which][way, k, :, first:first + lanes] = total.astype(BF16)
                chain_copy(way, k, n).start()

    chain_step(0)

    mod_here = mod[0, pl.ds(clip, 1)].reshape(3, WIDTH)
    scale = 1.0 + mod_here[1:2]
    mine = pl.ds(pl.multiple_of(spot * 16, 16), 16)

    def tokens_back(d, carry):
        b = back[d].astype(F32).reshape(64, WIDTH)
        b = jnp.stack(
            [
                jnp.concatenate([b[16 * g + 8 * f:16 * g + 8 * f + 8] for g in range(CHUNKS)], 0)
                for f in range(2)
            ],
            0,
        )
        rows = pl.ds(pl.multiple_of(lax.rem(spot + 8 - d, 8) * 32, 32), 32)
        normed, rstd = normalise(tok[0, :, rows, :].astype(F32))
        d_normed = b * scale
        one = jnp.mean(d_normed, -1, keepdims=True)
        two = jnp.mean(d_normed * normed, -1, keepdims=True)
        out = dout[0, :, rows, :].astype(F32) + rstd * (d_normed - one - normed * two)
        d_tok[0, :, rows, :] = out.astype(BF16)
        return (
            carry[0] + jnp.sum(b.reshape(8, 8, WIDTH), 0),
            carry[1] + jnp.sum((b * normed).reshape(8, 8, WIDTH), 0),
        )

    zero = jnp.zeros((8, WIDTH), F32)
    back[0] = d_in[:, mine, :]
    sums = tokens_back(0, (zero, zero))
    chain_step(1)
    for d in range(1, 8):
        back_copy(d).wait_recv()
    sums = lax.fori_loop(1, 8, tokens_back, sums)
    part[0:1] = jnp.sum(sums[0], 0, keepdims=True)
    part[1:2] = jnp.sum(sums[1], 0, keepdims=True)
    part[2:3] = gate_part[...]
    part[3:] = jnp.zeros((5, WIDTH), F32)

    def part_copy(d):
        return pltpu.make_async_remote_copy(
            src_ref=part, dst_ref=parts.at[d], send_sem=p_send.at[d],
            recv_sem=p_recv.at[d], device_id=peer(d), device_id_type=MESH,
        )

    for d in range(1, 8):
        part_copy(d).start()
    chain_step(2)
    total = part[...]
    for d in range(1, 8):
        part_copy(d).wait_recv()
        total = total + parts[d]
    d_mod[0, pl.ds(clip, 1)] = total[0:3].reshape(1, 3, WIDTH)

    def mod_copy(d):
        return pltpu.make_async_remote_copy(
            src_ref=d_mod.at[0, clip], dst_ref=d_mod.at[0, clip], send_sem=z_send.at[d],
            recv_sem=z_recv.at[d], device_id=along(d), device_id_type=MESH,
        )

    for d in range(1, 8):
        mod_copy(d).start()
    chain_step(3)
    for copy in pair_copies(7):
        copy.wait_recv()
    sums_ = []
    for which in range(2):
        whole = []
        for n, (which_n, first, lanes) in enumerate(PIECES):
            if which_n == which:
                total = own(which, clip, first, lanes)
                for way in range(2):
                    total = total + arrived(way, 3, n)
                whole.append(total.astype(BF16))
        sums_.append(jnp.concatenate(whole, 1))

    def widen(x, size, slot):
        count = 8 * slot
        row = lax.broadcasted_iota(jnp.int32, (count, x.shape[0]), 0)
        col = lax.broadcasted_iota(jnp.int32, (count, x.shape[0]), 1)
        inside = lax.rem(row, slot)
        pick = jnp.logical_and(col == lax.div(row, slot) * size + inside, inside < size)
        return dot(pick.astype(F32).astype(BF16), x, (1, 0)).astype(BF16)

    wide_q, wide_o = widen(sums_[0], 18, 32), widen(sums_[1], 9, 16)
    for j in range(8):
        for low in range(2):
            stage[j, low, 0:32, :] = wide_q[32 * j:32 * j + 32, 384 * low:384 * low + 512]
            stage[j, low, 32:48, 0:384] = wide_o[16 * j:16 * j + 16, 256 * low:256 * low + 384]
            stage[j, low, 32:48, 384:512] = jnp.zeros((16, 128), BF16)

    def owner_copy(d, low):
        to = half * 8 + d
        return pltpu.make_async_remote_copy(
            src_ref=stage.at[lax.rem(spot + d, 8), low], dst_ref=final.at[to],
            send_sem=f_send.at[d, low], recv_sem=f_recv.at[to],
            device_id=owner(d, low), device_id_type=MESH,
        )

    for d in range(1, 8):
        for low in range(2):
            owner_copy(d, low).start()
    for low in range(2):
        is_self = jnp.logical_and(core == half, core == low)

        @pl.when(is_self)
        def _():
            pltpu.make_async_copy(stage.at[spot, low], final.at[half * 8], f_recv.at[half * 8]).start()

        @pl.when(jnp.logical_not(is_self))
        def _():
            owner_copy(0, low).start()

    for i in range(16):
        wait_bytes(final.at[i], f_recv.at[i])
    total = final[0].astype(F32)
    for i in range(1, 16):
        total = total + final[i].astype(F32)
    got_q = jnp.where(core == 0, total[0:32, 0:SHARD_Q], total[0:32, 48:48 + SHARD_Q])
    first_o = 64 * half + 32 * core
    got_o = total[32:48, 0:SHARD_O]
    for start in (32, 64, 96):
        got_o = jnp.where(first_o == start, total[32:48, start:start + SHARD_O], got_o)
    got_q = jnp.concatenate([jnp.concatenate([got_q, jnp.zeros((32, 80), F32)], 1), jnp.zeros((96, 512), F32)], 0)
    got_o = jnp.concatenate([jnp.concatenate([got_o, jnp.zeros((16, 96), F32)], 1), jnp.zeros((112, 384), F32)], 0)
    oq[...] = got_q.T[0:SHARD_Q, 0:18]
    oo[...] = got_o.T[0:SHARD_O, 0:9]

    for d in range(1, 8):
        mod_copy(d).wait()
        back_copy(d).wait_send()
        part_copy(d).wait_send()
        for low in range(2):
            owner_copy(d, low).wait_send()
    for low in range(2):
        @pl.when(jnp.logical_or(core != half, core != low))
        def _():
            owner_copy(0, low).wait_send()
    for i in range(8):
        for copy in pair_copies(i):
            copy.wait_send()
    for k in range(STEPS):
        for way in range(2):
            for n in pieces(k, way):
                chain_copy(way, k, n).wait_send()


def call(kernel, outs, scratch, count, collective_id=None):
    params = dict(vmem_limit_bytes=VMEM_BYTES)
    if collective_id is not None:
        params.update(collective_id=collective_id, has_side_effects=True)
    whole = pl.BlockSpec(memory_space=pltpu.VMEM)
    return pl.pallas_call(
        kernel,
        out_shape=[jax.ShapeDtypeStruct(shape, dtype) for shape, dtype in outs],
        in_specs=[whole] * count,
        out_specs=[whole] * len(outs),
        scratch_shapes=scratch,
        compiler_params=pltpu.CompilerParams(**params),
    )


def body(tokens, d_out, modulation, w_qkv, w_out):
    dma = pltpu.SemaphoreType.DMA
    vmem = pltpu.VMEM
    moved = (CHUNKS, CHUNK, WIDTH)
    m_all, d_all, wq_all, wo_all = call(
        spread_kernel,
        [(moved, BF16), (moved, BF16), ((2 * HALF_Q, WIDTH), BF16), ((WIDTH, HEADS * HD), BF16)],
        [
            vmem((8, CHUNKS, 16, WIDTH), BF16), vmem((8, CHUNKS, 16, WIDTH), BF16),
            dma((2, 8)), dma((2, 8)), dma((6,)), dma((6,)), dma((2,)),
        ],
        5, 0,
    )(tokens, d_out, modulation, w_qkv, w_out)
    d_in, gq, go, gate_part = call(
        middle_kernel,
        [
            (moved, BF16), ((2, WIDTH, HALF_Q), BF16),
            ((2, HEADS * SLOT_E, HALF_O), BF16), ((1, WIDTH), F32),
        ],
        [
            vmem((ROWS, 2 * HALF_Q), BF16), vmem((ROWS, HEADS * HD), BF16),
            vmem((ROWS, HEADS * HD), BF16), vmem((ROWS, HEADS * SLOT_E), BF16),
            vmem((ROWS, WIDTH), BF16), vmem((ROWS, 2 * HALF_Q), BF16), vmem((WIDTH, ROWS), BF16),
        ],
        5,
    )(m_all, d_all, wq_all, wo_all, modulation)
    return call(
        finish_kernel,
        [
            (tokens.shape, BF16), (modulation.shape, F32),
            ((SHARD_Q, 18), F32), ((SHARD_O, 9), F32),
        ],
        [
            vmem((8, CHUNKS, 16, WIDTH), BF16),
            vmem((WIDTH, HALF_Q), BF16), vmem((HEADS * SLOT_E, HALF_O), BF16),
            vmem((2, STEPS, BLOCK_Q, HALF_Q), BF16), vmem((2, STEPS, BLOCK_O, HALF_O), BF16),
            vmem((2, STEPS, BLOCK_Q, HALF_Q), BF16), vmem((2, STEPS, BLOCK_O, HALF_O), BF16),
            vmem((8, 2, 48, 512), BF16), vmem((16, 48, 512), BF16),
            vmem((8, WIDTH), F32), vmem((8, 8, WIDTH), F32),
            dma((8,)), dma((8,)), dma((8, 2)), dma((8, 2)),
            dma((2, STEPS, len(PIECES))), dma((2, STEPS, len(PIECES))),
            dma((8,)), dma((8,)), dma((8,)), dma((8,)), dma((8, 2)), dma((16,)),
        ],
        7, 1,
    )(d_in, gq, go, gate_part, tokens, d_out, modulation)


def solution(mesh):
    in_specs = (
        P("dp", "seq", None, None),
        P("dp", "seq", None, None),
        P("dp", None, None, None),
        P("dp", None),
        P("dp", None),
    )
    out_specs = (
        P("dp", "seq", None, None),
        P("dp", None, None, None),
        P("dp", "seq"),
        P("dp", "seq"),
    )
    return jax.shard_map(body, mesh=mesh, in_specs=in_specs, out_specs=out_specs, check_vma=False)
```

time: 1190 us -> 168 us (0.14)
  waiting for transfers between devices: 471 us -> 0 us
  blocking collectives: 443 us -> 0 us
  Pallas kernels: 0 us -> 158 us
  starting transfers between devices: 80.7 us -> 0 us
  local copies, waits for them, and re-layouts: 89.1 us -> 8.83 us
  matrix products: 46.4 us -> 0 us
  other arithmetic: 34.7 us -> 0 us
  between operations: 16 us -> 0.65 us
    psum x1 -> x0, waiting for transfers between devices: 352 us -> none  [body(): local_sum = lax.psum(local_part, 'seq')]
    psum x1 -> x0, blocking collectives: 252 us -> none  [body(): gate_sum = lax.psum(gate_part, 'seq')]
    unnamed x1 -> x0, blocking collectives: 191 us -> none
    pallas_call x0 -> x3, Pallas kernels: none -> 158 us  [the longest x1 69.4 us: body(): call(finish_kernel, [(tokens.shape, BF16), (modulation.shape, F32), ((SHA...]
    unnamed x23 -> x0, waiting for transfers between devices: 74.3 us -> none
    unnamed x18 -> x0, starting transfers between devices: 48.4 us -> none
    dot_general x11 -> x0, matrix products: 41.7 us -> none  [the longest x2 10.9 us: matmul_tokens(): lax.dot_general(left, right, (((0,), (0,)), ((), ())), preferred_element_...]
    unnamed x67 -> x2, local copies, waits for them, and re-layouts: 45 us -> 3.97 us
  transfers between devices with their start and end apart: 24 -> 0, of which waited for: 5 -> 0; matrix products, arithmetic and copies ran while one was open for 25% -> 0% of each run, Pallas kernels for 0% -> 0%
where the time goes in v1:
time: 168 us
  Pallas kernels  158 us (94%)
  local copies, waits for them, and re-layouts  8.83 us (5%)
    pallas_call x1, Pallas kernels, body(): call(finish_kernel, [(tokens.shape, BF16), (modulation.shape, F32), ((SHA...  69.4 us
    pallas_call x1, Pallas kernels, body(): call(spread_kernel, [(moved, BF16), (moved, BF16), ((2 * HALF_Q, WIDTH),...  45.6 us
    pallas_call x1, Pallas kernels, body(): call(middle_kernel, [(moved, BF16), ((2, WIDTH, HALF_Q), BF16), ((2, HEAD...  43.5 us
    pallas_call x3, local copies, waits for them, and re-layouts, body(): call(finish_kernel, [(tokens.shape, BF16), (modulation.shape, F32), ((SHA...  4.86 us
    unnamed x2, local copies, waits for them, and re-layouts  3.97 us

profile of v1, /device:TPU:1, one launch (start us, length us, event | category | flops | bytes accessed | tf_op | source)
XLA Modules:
  0.0 167.9 jit_solution(5187686070602755608)
XLA Ops:
  0.6 1.6 copy.9.mod
  2.2 45.6 %shard_map.84 = (bf16[4,128,1152]{2,1,0:T(8,128)(2,1)}, bf16[4,128,1152]{2,1,0:T(8,128)(2,1)}, bf16[1792,1152]{1,0:T(8,128)(2,1)}, bf16[1152,576]{1,0:T(8,128)(2,1)}) custom-call(bf16[1,2,256,1152]{3,2,1,0:T(8,128)(2,1)} %tok.3, bf16[1,2,256,1152]{3,2,1,0:T(8,128)(2,1)} %dout.3, f32[1,8,3,1152]{3,2,1,0:T(4,128)} %copy.9.mod, bf16[432,1152]{1,0:T(8,128)(2,1)} %wq.1, ...), custom_call_target="tpu_custom_call" | custom-call | tf_op jit(solution)/shard_map/pallas_call | solution.py:514
  47.8 43.5 %shard_map.85 = (bf16[4,128,1152]{2,1,0:T(8,128)(2,1)}, bf16[2,1152,896]{2,1,0:T(8,128)(2,1)}, bf16[2,640,640]{2,1,0:T(8,128)(2,1)}, f32[1,1152]{1,0:T(1,128)}) custom-call(bf16[4,128,1152]{2,1,0:T(8,128)(2,1)} %get-tuple-element.12.m_all, bf16[4,128,1152]{2,1,0:T(8,128)(2,1)} %get-tuple-element.13.d_all, bf16[1792,1152]{1,0:T(8,128)(2,1)} %get-tuple-element.14.wq_all, ...), custom_call_target="tpu_custom_call" | custom-call | tf_op jit(solution)/shard_map/pallas_call | solution.py:523
  91.3 69.4 %shard_map.86 = (bf16[1,2,256,1152]{3,2,1,0:T(8,128)(2,1)}, f32[1,8,3,1152]{3,2,1,0:T(4,128)}, f32[432,18]{1,0:T(8,128)}, f32[288,9]{1,0:T(8,128)}) custom-call(bf16[4,128,1152]{2,1,0:T(8,128)(2,1)} %get-tuple-element.16.d_in, bf16[2,1152,896]{2,1,0:T(8,128)(2,1)} %get-tuple-element.17.gq, bf16[2,640,640]{2,1,0:T(8,128)(2,1)} %get-tuple-element.18.go, ...), custom_call_target="tpu_custom_call" | custom-call | tf_op jit(solution)/shard_map/pallas_call | solution.py:536
  160.7 1.6 copy.14
  162.3 1.7 copy.13
  164.0 1.6 copy.12
  165.5 2.4 %copy.16 = bf16[1,2,256,1152]{3,2,1,0:T(8,128)(2,1)} copy(bf16[1,2,256,1152]{3,2,1,0:T(8,128)(2,1)} %get-tuple-element.28) | data formatting | bytes 2359296

commit v2 on v0

v2 whole, which is shorter than its diff:
```python
import math

import jax
import jax.numpy as jnp
from jax import lax
from jax.experimental import pallas as pl
from jax.experimental.pallas import tpu as pltpu
from jax.sharding import PartitionSpec as P

MESH = pl.DeviceIdType.MESH
F32 = jnp.float32
BF16 = jnp.bfloat16

WIDTH = 1152
HEADS = 8
HD = 72
FRAMES = 16
CLIP_DEVICES = 8
CHUNKS = 4
CHUNK = 128
ROWS = 512
SHARD_Q = 432
SHARD_O = 288
HALF_Q = 896
HALF_O = 640
START_O = 512
SLOT_E = 80
EPS = 1e-06
VMEM_BYTES = 56 * 1024 * 1024

PIECES = ((0, 0, 512), (0, 512, 384), (1, 0, 256), (1, 256, 384))
FIRST_PIECES = ((0, 2), (1, 3))
BLOCK_Q = 144
BLOCK_O = SLOT_E
OFFSETS = (4, 3, 5, 2, 6, 1, 7, 0)
STEPS = 4
HALF_ROWS = 256

PIECES_WQ = (((0, 64), (64, 48), (112, 64), (176, 48)), ((224, 64), (288, 48), (336, 48), (384, 48)))
PIECES_WO = (((0, 48), (48, 32), (80, 32), (112, 32)), ((144, 48), (192, 32), (224, 32), (256, 32)))


def dot(left, right, contract):
    return lax.dot_general(
        left, right, ((contract[:1], contract[1:]), ((), ())), preferred_element_type=F32
    )


def place():
    seq, dp = lax.axis_index("seq"), lax.axis_index("dp")
    clip, spot = lax.div(seq, 8), lax.rem(seq, 8)
    half, core = lax.div(dp, 2), lax.rem(dp, 2)
    return seq, dp, clip, spot, half, core


def column(part, head):
    block = part * HEADS + head
    return block * HD if block < 12 else HALF_Q + (block - 12) * HD


def normalise(x):
    center = x - jnp.mean(x, -1, keepdims=True)
    var = jnp.mean(center * center, -1, keepdims=True)
    rstd = lax.rsqrt(var + EPS)
    return center * rstd, rstd


def signal_all(barrier, devices):
    for device in devices:
        pl.semaphore_signal(barrier, inc=1, device_id=device, device_id_type=MESH)


def by_parity(clip, act):
    for parity in range(2):
        @pl.when(lax.rem(clip, 2) == parity)
        def _():
            act(parity)


def wait_bytes(ref, sem):
    pltpu.make_async_copy(ref, ref, sem).wait()


def fused_kernel(
    tok_in, dout_in, mod, wq, wo, tok_out, d_mod, oq, oo,
    tok, dout, m_send, d_send, m_all, d_all, wq_all, wo_all,
    qkv, datt, att, att_slots, dbranch, dqkv, turned, d_in, gq, go,
    back, xq, xo, sq, so, rq, ro, stage, final, part, parts, mods,
    here, a_send, a_recv, own_send, own_recv, w_send, w_recv, v_send, v_recv, t_send, t_recv,
    b_send, b_recv, x_send, x_recv, c_send, c_recv, p_send, p_recv,
    z_send, z_recv, f_send, f_recv,
):
    seq, dp, clip, spot, half, core = place()
    twin = {"seq": seq, "dp": half * 2 + 1 - core}
    across = {
        "seq": clip * 8 + (1 - lax.div(spot, 4)) * 4 + lax.rem(spot, 4),
        "dp": (1 - half) * 2 + core,
    }

    def peer(d):
        return {"seq": clip * 8 + lax.rem(spot + d, 8), "dp": dp}

    def along(d):
        return {"seq": lax.rem(clip + d, 8) * 8 + spot, "dp": dp}

    def owner(d, low):
        return {"seq": clip * 8 + lax.rem(spot + d, 8), "dp": core * 2 + low}

    def source(d, h):
        return {"seq": clip * 8 + lax.rem(spot + 8 - d, 8), "dp": h * 2 + half}

    def remote(src, dst, send, recv, device):
        return pltpu.make_async_remote_copy(
            src_ref=src, dst_ref=dst, send_sem=send, recv_sem=recv,
            device_id=device, device_id_type=MESH,
        )

    loads = [
        pltpu.make_async_copy(tok_in.at[0], tok, here.at[0]),
        pltpu.make_async_copy(dout_in.at[0], dout, here.at[1]),
    ]
    for copy in loads:
        copy.start()
    barrier = pltpu.get_barrier_semaphore()
    signal_all(barrier, [twin, across] + [peer(d) for d in range(1, 8)] + [along(d) for d in range(1, 8)])
    signal_all(barrier, [source(d, h) for d in range(1, 8) for h in range(2)])
    for h in range(2):
        @pl.when(jnp.logical_or(half != core, h != half))
        def _():
            signal_all(barrier, [source(0, h)])
    pl.semaphore_wait(barrier, jnp.where(half == core, 31, 32))

    shards, wholes = (wq, wo), (wq_all, wo_all)

    def first_row(n, h, c):
        return h * HALF_Q + c * SHARD_Q if n == 0 else (h * 2 + c) * SHARD_O

    def rows(n, h, c, at):
        return wholes[n].at[pl.ds(pl.multiple_of(first_row(n, h, c) + at[0], 16), at[1])]

    def entire(n):
        return (0, (SHARD_Q, SHARD_O)[n])

    def piece(n, parity, i):
        return (PIECES_WQ, PIECES_WO)[n][parity][i]

    def own_copy(n):
        return remote(shards[n], rows(n, half, core, entire(n)), own_send.at[n], own_recv.at[n], twin)

    def keep_copy(n):
        return pltpu.make_async_copy(shards[n], rows(n, half, core, entire(n)), here.at[2 + n])

    def across_copy(n, parity, i):
        at = piece(n, parity, i)
        return remote(
            shards[n].at[pl.ds(at[0], at[1])], rows(n, half, core, at),
            w_send.at[n, i], w_recv.at[n, i], across,
        )

    def passed(n, parity, i):
        return rows(n, 1 - half, core, piece(n, parity, i))

    def along_copy(n, parity, i):
        ref = passed(n, parity, i)
        return remote(ref, ref, v_send.at[n, i], v_recv.at[n, i], along(1 if i % 2 == 0 else 7))

    def twin_copy(n, parity, i, own):
        ref = passed(n, parity, i)
        return remote(ref, ref, t_send.at[n, i, own], t_recv.at[n, i, own], twin)

    def send_across(parity):
        for i in range(4):
            for n in range(2):
                across_copy(n, parity, i).start()

    by_parity(clip, send_across)
    for n in range(2):
        keep_copy(n).start()
        own_copy(n).start()
    zeros = jnp.zeros((HALF_Q - 2 * SHARD_Q, WIDTH), BF16)
    wq_all[2 * SHARD_Q:HALF_Q, :] = zeros
    wq_all[HALF_Q + 2 * SHARD_Q:, :] = zeros

    own_mod = mod[0, :, pl.ds(clip, 1), :].reshape(3, WIDTH)
    shift, scale, gate = own_mod[0:1], 1.0 + own_mod[1:2], own_mod[2:3]
    mine = pl.ds(pl.multiple_of(spot * 16, 16), 16)

    def arranged(x):
        return jnp.concatenate(
            [x[f, 8 * g:8 * g + 8] for g in range(2) for f in range(2)], 0
        ).astype(BF16).reshape(2, 16, WIDTH)

    def patches(part, j):
        return pl.ds(pl.multiple_of(j * 32 + part * 16, 16), 16)

    def blocks(part, d):
        at = patches(part, lax.rem(spot + d, 8))
        normed, _ = normalise(tok[:, at, :].astype(F32))
        return arranged(normed * scale + shift), arranged(dout[:, at, :].astype(F32))

    def spread_copies(part, d):
        return [
            remote(
                src.at[part, d], dst.at[2 * part:2 * part + 2, mine, :],
                a_send.at[i, part, d], a_recv.at[i, part, d], peer(d),
            )
            for i, (src, dst) in enumerate(((m_send, m_all), (d_send, d_all)))
        ]

    for copy in loads:
        copy.wait()
    for part_ in range(2):
        @pl.loop(1, 8)
        def _(d):
            m_send[part_, d], d_send[part_, d] = blocks(part_, d)
            for copy in spread_copies(part_, d):
                copy.start()

        at = slice(2 * part_, 2 * part_ + 2)
        m_all[at, mine, :], d_all[at, mine, :] = blocks(part_, 0)

    for ref, start in ((dqkv, 2 * SHARD_Q), (dqkv, HALF_Q + 2 * SHARD_Q)):
        ref[:, start:start + 32] = jnp.zeros((ROWS, 32), BF16)
    att_slots[...] = jnp.zeros_like(att_slots)

    for i in range(4):
        def hand_on(parity):
            for n in range(2):
                across_copy(n, parity, i).wait_recv()
                along_copy(n, parity, i).start()
                twin_copy(n, parity, i, 0).start()

        by_parity(clip, hand_on)
    for i in range(4):
        def hand_twin(parity):
            for n in range(2):
                along_copy(n, 1 - parity, i).wait_recv()
                twin_copy(n, 1 - parity, i, 1).start()

        by_parity(clip, hand_twin)
    for n in range(2):
        keep_copy(n).wait()
        own_copy(n).wait_recv()

    def from_twin(parity):
        for i in range(4):
            for n in range(2):
                twin_copy(n, parity, i, 0).wait_recv()
                twin_copy(n, 1 - parity, i, 1).wait_recv()

    by_parity(clip, from_twin)

    inv = 1.0 / math.sqrt(HD)
    kept = (
        lax.broadcasted_iota(jnp.int32, (1, 8, CHUNK), 1)
        == lax.rem(lax.broadcasted_iota(jnp.int32, (1, 8, CHUNK), 2), 8)
    ).astype(F32)

    def attention(at):
        cols = [[column(part, h) for part in range(3)] for h in range(HEADS)]
        q, k, v = (
            [qkv[at, cols[h][part]:cols[h][part] + HD] for h in range(HEADS)] for part in range(3)
        )
        da = [datt[at, h * HD:h * HD + HD] for h in range(HEADS)]
        scores = [dot(k[h], q[h], (1, 1)) for h in range(HEADS)]
        d_probs = [dot(v[h], da[h], (1, 1)) for h in range(HEADS)]
        probs_b, d_scores = [], []
        for h in range(HEADS):
            x = (scores[h] * inv).reshape(FRAMES, 8, CHUNK)
            e = jnp.exp(x - jnp.max(x, 0, keepdims=True))
            probs = e * (kept / jnp.sum(e, 0, keepdims=True))
            probs_b.append(probs.astype(BF16).reshape(CHUNK, CHUNK))
            dp_ = d_probs[h].reshape(FRAMES, 8, CHUNK)
            spread = jnp.sum(probs * dp_, 0, keepdims=True)
            d_scores.append((probs * (dp_ - spread) * inv).astype(BF16).reshape(CHUNK, CHUNK))
        attended = [dot(probs_b[h], v[h], (0, 0)).astype(BF16) for h in range(HEADS)]
        d_q = [dot(d_scores[h], k[h], (0, 0)).astype(BF16) for h in range(HEADS)]
        d_k = [dot(d_scores[h], q[h], (1, 0)).astype(BF16) for h in range(HEADS)]
        d_v = [dot(probs_b[h], da[h], (1, 0)).astype(BF16) for h in range(HEADS)]
        for h in range(HEADS):
            att[at, h * HD:h * HD + HD] = attended[h]
            att_slots[at, h * SLOT_E:h * SLOT_E + HD] = attended[h]
            for part, grad in enumerate((d_q, d_k, d_v)):
                dqkv[at, cols[h][part]:cols[h][part] + HD] = grad[h]

    def back_copy(part, d):
        to = pl.ds(pl.multiple_of(lax.rem(spot + d, 8) * 16, 16), 16)
        at = slice(2 * part, 2 * part + 2)
        return remote(
            d_in.at[at, to, :], back.at[part, d], b_send.at[part, d], b_recv.at[part, d], peer(d)
        )

    for part_ in range(2):
        for d in range(1, 8):
            for copy in spread_copies(part_, d):
                copy.wait_recv()
        two = slice(2 * part_, 2 * part_ + 2)
        at = slice(part_ * HALF_ROWS, part_ * HALF_ROWS + HALF_ROWS)
        m = m_all[two].reshape(HALF_ROWS, WIDTH)
        qkv[at, :] = dot(m, wq_all[...], (1, 1)).astype(BF16)
        dbranch[at, :] = (gate * d_all[two].reshape(HALF_ROWS, WIDTH).astype(F32)).astype(BF16)
        datt[at, :] = dot(dbranch[at, :], wo_all[...], (1, 0)).astype(BF16)

        @pl.loop(2 * part_, 2 * part_ + 2)
        def _(c):
            attention(pl.ds(pl.multiple_of(c * CHUNK, CHUNK), CHUNK))

        for n in range(3):
            lanes = slice(n * 384, n * 384 + 384)
            grad = dot(dqkv[at, :], wq_all[:, lanes], (1, 0)).astype(BF16)
            d_in[two, :, lanes] = grad.reshape(2, CHUNK, 384)
        for d in range(1, 8):
            back_copy(part_, d).start()

    def block(size, z):
        return pl.ds(pl.multiple_of(z * size, 16), size)

    sizes = (BLOCK_Q, BLOCK_O)
    terms, theirs = (gq, go), (xq, xo)

    def pair_copy(i, n):
        at = block(sizes[n], lax.rem(clip + OFFSETS[i], 8))
        return remote(
            terms[n].at[1 - core, at, :], theirs[n].at[at, :], x_send.at[i, n], x_recv.at[i, n], twin
        )

    turned[...] = m_all[...].reshape(ROWS, WIDTH).T
    slots = att_slots[...].T

    def weight_terms(h):
        go[h] = dot(slots, dbranch[:, pl.ds(pl.multiple_of(h * START_O, 128), HALF_O)], (1, 0)).astype(BF16)
        for first, lanes in ((0, 512), (512, 384)):
            src = pl.ds(pl.multiple_of(h * HALF_Q + first, 128), lanes)
            gq[h, :, first:first + lanes] = dot(turned[...], dqkv[:, src], (1, 0)).astype(BF16)

    weight_terms(1 - core)
    for i in range(8):
        for n in range(2):
            pair_copy(i, n).start()
    weight_terms(core)

    def own(which, z, first, lanes):
        at = block(sizes[which], z)
        return (
            terms[which][core, at, first:first + lanes].astype(F32)
            + theirs[which][at, first:first + lanes].astype(F32)
        )

    def pieces(k, way):
        return FIRST_PIECES[way] if k == 0 else range(len(PIECES))

    def chain_copy(way, k, n):
        which, first, lanes = PIECES[n]
        src, dst = ((sq, rq), (so, ro))[which]
        return remote(
            src.at[way, k, :, first:first + lanes], dst.at[way, k, :, first:first + lanes],
            c_send.at[way, k, n], c_recv.at[way, k, n], along(1 if way == 0 else 7),
        )

    def arrived(way, k, n):
        which, first, lanes = PIECES[n]
        chain_copy(way, k, n).wait_recv()
        return (rq, ro)[which][way, k, :, first:first + lanes].astype(F32)

    def chain_step(k):
        for i in (0,) if k == 0 else (2 * k - 1, 2 * k):
            for n in range(2):
                pair_copy(i, n).wait_recv()
        for n in range(len(PIECES)):
            for way in range(2):
                if n not in pieces(k, way):
                    continue
                which, first, lanes = PIECES[n]
                z = lax.rem(clip + (4 - k if way == 0 else 4 + k), 8)
                total = own(which, z, first, lanes)
                if k and n in pieces(k - 1, way):
                    total = total + arrived(way, k - 1, n)
                (sq, so)[which][way, k, :, first:first + lanes] = total.astype(BF16)
                chain_copy(way, k, n).start()

    chain_step(0)

    gates = []
    for n in range(3):
        lanes = slice(n * 384, n * 384 + 384)
        branch = dot(att[...], wo_all[lanes, :], (1, 1))
        grads = d_all[:, :, lanes].reshape(ROWS, 384).astype(F32)
        gates.append(jnp.sum(branch * grads, 0, keepdims=True))
    part[2:3] = jnp.concatenate(gates, 1)
    part[3:] = jnp.zeros((5, WIDTH), F32)

    def tokens_back(half_):
        def step(d, carry):
            b = back[half_, d].astype(F32).reshape(32, WIDTH)
            b = jnp.stack(
                [
                    jnp.concatenate([b[16 * g + 8 * f:16 * g + 8 * f + 8] for g in range(2)], 0)
                    for f in range(2)
                ],
                0,
            )
            at = patches(half_, lax.rem(spot + 8 - d, 8))
            normed, rstd = normalise(tok[:, at, :].astype(F32))
            d_normed = b * scale
            one = jnp.mean(d_normed, -1, keepdims=True)
            two = jnp.mean(d_normed * normed, -1, keepdims=True)
            out = dout[:, at, :].astype(F32) + rstd * (d_normed - one - normed * two)
            dout[:, at, :] = out.astype(BF16)
            return (
                carry[0] + jnp.sum(b.reshape(4, 8, WIDTH), 0),
                carry[1] + jnp.sum((b * normed).reshape(4, 8, WIDTH), 0),
            )

        return step

    zero = jnp.zeros((8, WIDTH), F32)
    sums = (zero, zero)
    for part_ in range(2):
        back[part_, 0] = d_in[2 * part_:2 * part_ + 2, mine, :]
        for d in range(1, 8):
            back_copy(part_, d).wait_recv()
        sums = lax.fori_loop(0, 8, tokens_back(part_), sums)
        if part_ == 0:
            chain_step(1)
    result = pltpu.make_async_copy(dout, tok_out.at[0], here.at[4])
    result.start()
    part[0:1] = jnp.sum(sums[0], 0, keepdims=True)
    part[1:2] = jnp.sum(sums[1], 0, keepdims=True)

    def part_copy(d):
        return remote(part, parts.at[d], p_send.at[d], p_recv.at[d], peer(d))

    for d in range(1, 8):
        part_copy(d).start()
    chain_step(2)
    total = part[...]
    for d in range(1, 8):
        part_copy(d).wait_recv()
        total = total + parts[d]
    mods[clip] = total

    def mod_copy(d):
        ref = mods.at[clip]
        return remote(ref, ref, z_send.at[d], z_recv.at[d], along(d))

    for d in range(1, 8):
        mod_copy(d).start()
    chain_step(3)
    for n in range(2):
        pair_copy(7, n).wait_recv()
    sums_ = []
    for which in range(2):
        whole = []
        for n, (which_n, first, lanes) in enumerate(PIECES):
            if which_n == which:
                total = own(which, clip, first, lanes)
                for way in range(2):
                    total = total + arrived(way, 3, n)
                whole.append(total.astype(BF16))
        sums_.append(jnp.concatenate(whole, 1))

    def widen(x, size, slot):
        count = 8 * slot
        row = lax.broadcasted_iota(jnp.int32, (count, x.shape[0]), 0)
        col = lax.broadcasted_iota(jnp.int32, (count, x.shape[0]), 1)
        inside = lax.rem(row, slot)
        pick = jnp.logical_and(col == lax.div(row, slot) * size + inside, inside < size)
        return dot(pick.astype(F32).astype(BF16), x, (1, 0)).astype(BF16)

    wide_q, wide_o = widen(sums_[0], 18, 32), widen(sums_[1], 9, 16)
    for j in range(8):
        for low in range(2):
            stage[j, low, 0:32, :] = wide_q[32 * j:32 * j + 32, 384 * low:384 * low + 512]
            stage[j, low, 32:48, 0:384] = wide_o[16 * j:16 * j + 16, 256 * low:256 * low + 384]
            stage[j, low, 32:48, 384:512] = jnp.zeros((16, 128), BF16)

    def owner_copy(d, low):
        to = half * 8 + d
        return pltpu.make_async_remote_copy(
            src_ref=stage.at[lax.rem(spot + d, 8), low], dst_ref=final.at[to],
            send_sem=f_send.at[d, low], recv_sem=f_recv.at[to],
            device_id=owner(d, low), device_id_type=MESH,
        )

    for d in range(1, 8):
        for low in range(2):
            owner_copy(d, low).start()
    for low in range(2):
        is_self = jnp.logical_and(core == half, core == low)

        @pl.when(is_self)
        def _():
            pltpu.make_async_copy(stage.at[spot, low], final.at[half * 8], f_recv.at[half * 8]).start()

        @pl.when(jnp.logical_not(is_self))
        def _():
            owner_copy(0, low).start()

    for i in range(16):
        wait_bytes(final.at[i], f_recv.at[i])
    total = final[0].astype(F32)
    for i in range(1, 16):
        total = total + final[i].astype(F32)
    got_q = jnp.where(core == 0, total[0:32, 0:SHARD_Q], total[0:32, 48:48 + SHARD_Q])
    first_o = 64 * half + 32 * core
    got_o = total[32:48, 0:SHARD_O]
    for start in (32, 64, 96):
        got_o = jnp.where(first_o == start, total[32:48, start:start + SHARD_O], got_o)
    oq[...] = got_q[0:18]
    oo[...] = got_o[0:9]

    for d in range(1, 8):
        mod_copy(d).wait()
        part_copy(d).wait_send()
        for part_ in range(2):
            back_copy(part_, d).wait_send()
            for copy in spread_copies(part_, d):
                copy.wait_send()
        for low in range(2):
            owner_copy(d, low).wait_send()
    for low in range(2):
        @pl.when(jnp.logical_or(core != half, core != low))
        def _():
            owner_copy(0, low).wait_send()
    for n in range(2):
        own_copy(n).wait_send()
        for i in range(8):
            pair_copy(i, n).wait_send()
    for k in range(STEPS):
        for way in range(2):
            for n in pieces(k, way):
                chain_copy(way, k, n).wait_send()

    def sent(parity):
        for i in range(4):
            for n in range(2):
                across_copy(n, parity, i).wait_send()
                along_copy(n, parity, i).wait_send()
                twin_copy(n, parity, i, 0).wait_send()
                twin_copy(n, 1 - parity, i, 1).wait_send()

    by_parity(clip, sent)
    for i in range(3):
        d_mod[0, i] = jnp.concatenate([mods[z, i:i + 1] for z in range(8)], 0)
    result.wait()


def copy_kernel(*refs):
    count = len(refs) // 2
    for i in range(count):
        refs[count + i][...] = refs[i][...]


def body(tokens, d_out, modulation, w_qkv, w_out):
    dma = pltpu.SemaphoreType.DMA

    def held(*shape, dtype=BF16):
        return pltpu.VMEM(shape, dtype)

    anywhere = pl.BlockSpec(memory_space=pl.ANY)
    inside = pl.BlockSpec(memory_space=pltpu.VMEM)
    outs = [
        jax.ShapeDtypeStruct(tokens.shape, BF16),
        jax.ShapeDtypeStruct((1, 3, 8, WIDTH), F32),
        jax.ShapeDtypeStruct((18, SHARD_Q), F32),
        jax.ShapeDtypeStruct((9, SHARD_O), F32),
    ]
    chains = (2, STEPS, len(PIECES))
    results = pl.pallas_call(
        fused_kernel,
        out_shape=outs,
        in_specs=[anywhere, anywhere, inside, anywhere, anywhere],
        out_specs=[anywhere, inside, inside, inside],
        scratch_shapes=[
            held(2, 256, WIDTH), held(2, 256, WIDTH),
            held(2, 8, 2, 16, WIDTH), held(2, 8, 2, 16, WIDTH),
            held(CHUNKS, CHUNK, WIDTH), held(CHUNKS, CHUNK, WIDTH),
            held(2 * HALF_Q, WIDTH), held(WIDTH, HEADS * HD),
            held(ROWS, 2 * HALF_Q), held(ROWS, HEADS * HD), held(ROWS, HEADS * HD),
            held(ROWS, HEADS * SLOT_E), held(ROWS, WIDTH), held(ROWS, 2 * HALF_Q),
            held(WIDTH, ROWS), held(CHUNKS, CHUNK, WIDTH),
            held(2, WIDTH, HALF_Q), held(2, HEADS * SLOT_E, HALF_O),
            held(2, 8, 2, 16, WIDTH), held(WIDTH, HALF_Q), held(HEADS * SLOT_E, HALF_O),
            held(2, STEPS, BLOCK_Q, HALF_Q), held(2, STEPS, BLOCK_O, HALF_O),
            held(2, STEPS, BLOCK_Q, HALF_Q), held(2, STEPS, BLOCK_O, HALF_O),
            held(8, 2, 48, 512), held(16, 48, 512),
            held(8, WIDTH, dtype=F32), held(8, 8, WIDTH, dtype=F32), held(8, 8, WIDTH, dtype=F32),
            dma((5,)), dma((2, 2, 8)), dma((2, 2, 8)), dma((2,)), dma((2,)),
            dma((2, 4)), dma((2, 4)), dma((2, 4)), dma((2, 4)), dma((2, 4, 2)), dma((2, 4, 2)),
            dma((2, 8)), dma((2, 8)), dma((8, 2)), dma((8, 2)), dma(chains), dma(chains),
            dma((8,)), dma((8,)), dma((8,)), dma((8,)), dma((8, 2)), dma((16,)),
        ],
        compiler_params=pltpu.CompilerParams(
            vmem_limit_bytes=VMEM_BYTES, collective_id=0, has_side_effects=True
        ),
    )(tokens, d_out, jnp.swapaxes(modulation, 1, 2), w_qkv, w_out)
    d_tokens, d_mod, g_qkv, g_out = pl.pallas_call(
        copy_kernel,
        out_shape=outs,
        in_specs=[inside] * 4,
        out_specs=[inside] * 4,
        compiler_params=pltpu.CompilerParams(vmem_limit_bytes=16 * 1024 * 1024),
    )(*results)
    return d_tokens, jnp.swapaxes(d_mod, 1, 2), g_qkv.T, g_out.T


def solution(mesh):
    in_specs = (
        P("dp", "seq", None, None),
        P("dp", "seq", None, None),
        P("dp", None, None, None),
        P("dp", None),
        P("dp", None),
    )
    out_specs = (
        P("dp", "seq", None, None),
        P("dp", None, None, None),
        P("dp", "seq"),
        P("dp", "seq"),
    )
    return jax.shard_map(body, mesh=mesh, in_specs=in_specs, out_specs=out_specs, check_vma=False)
```

time: 1190 us -> 114 us (0.10)
  waiting for transfers between devices: 471 us -> 0 us
  blocking collectives: 443 us -> 0 us
  Pallas kernels: 0 us -> 109 us
  local copies, waits for them, and re-layouts: 89.1 us -> 3.69 us
  starting transfers between devices: 80.7 us -> 0 us
  matrix products: 46.4 us -> 0 us
  other arithmetic: 34.7 us -> 0 us
  between operations: 16 us -> 0.65 us
    psum x1 -> x0, waiting for transfers between devices: 352 us -> none  [body(): local_sum = lax.psum(local_part, 'seq')]
    psum x1 -> x0, blocking collectives: 252 us -> none  [body(): gate_sum = lax.psum(gate_part, 'seq')]
    unnamed x1 -> x0, blocking collectives: 191 us -> none
    pallas_call x0 -> x2, Pallas kernels: none -> 109 us  [the longest x1 108 us: body(): pl.pallas_call(fused_kernel, out_shape=outs, in_specs=[anywhere, anywhere...]
    unnamed x23 -> x0, waiting for transfers between devices: 74.3 us -> none
    unnamed x18 -> x0, starting transfers between devices: 48.4 us -> none
    dot_general x11 -> x0, matrix products: 41.7 us -> none  [the longest x2 10.9 us: matmul_tokens(): lax.dot_general(left, right, (((0,), (0,)), ((), ())), preferred_element_...]
    unnamed x67 -> x8, local copies, waits for them, and re-layouts: 45 us -> 3.69 us
  transfers between devices with their start and end apart: 24 -> 0, of which waited for: 5 -> 0; matrix products, arithmetic and copies ran while one was open for 25% -> 0% of each run, Pallas kernels for 0% -> 0%
where the time goes in v2:
time: 114 us
  Pallas kernels  109 us (96%)
  local copies, waits for them, and re-layouts  3.69 us (3%)
    pallas_call x1, Pallas kernels, body(): pl.pallas_call(fused_kernel, out_shape=outs, in_specs=[anywhere, anywhere...  108 us
    unnamed x8, local copies, waits for them, and re-layouts  3.69 us

profile of v2, /device:TPU:1, one launch (start us, length us, event | category | flops | bytes accessed | tf_op | source)
XLA Modules:
  0.0 113.5 jit_solution(552632748371788615)
XLA Ops:
  0.6 108.0 %shard_map.84 = (bf16[1,2,256,1152]{3,2,1,0:T(8,128)(2,1)}, f32[1,3,8,1152]{3,2,1,0:T(8,128)}, f32[18,432]{1,0:T(8,128)}, f32[9,288]{1,0:T(8,128)}) custom-call(bf16[1,2,256,1152]{3,2,1,0:T(8,128)(2,1)} %tok_in.1, bf16[1,2,256,1152]{3,2,1,0:T(8,128)(2,1)} %dout_in.1, f32[1,3,8,1152]{3,2,1,0:T(8,128)} %bitcast.4, bf16[432,1152]{1,0:T(8,128)(2,1)} %wq.1, ...), custom_call_target="tpu_custom_call" | custom-call | tf_op jit(solution)/shard_map/pallas_call | solution.py:569
  108.7 0.0 copy-start
  108.7 1.3 %copy-done = bf16[1,2,256,1152]{3,2,1,0:T(8,128)(2,1)S(1)} copy-done((bf16[1,2,256,1152]{3,2,1,0:T(8,128)(2,1)S(1)}, bf16[1,2,256,1152]{3,2,1,0:T(8,128)(2,1)}, u32[]{:S(2)}) %copy-start) | copy-done | bytes 1179672
  110.0 0.0 copy-start.1
  110.0 0.9 copy-done.1
  110.9 0.0 copy-start.2
  110.9 0.8 copy-done.2
  111.7 0.0 copy-start.3
  111.7 0.7 copy-done.3
  112.4 1.1 %shard_map.85 = (bf16[1,2,256,1152]{3,2,1,0:T(8,128)(2,1)}, f32[1,3,8,1152]{3,2,1,0:T(8,128)}, f32[18,432]{1,0:T(8,128)}, f32[9,288]{1,0:T(8,128)}) custom-call(bf16[1,2,256,1152]{3,2,1,0:T(8,128)(2,1)S(1)} %copy-done, f32[1,3,8,1152]{3,2,1,0:T(8,128)S(1)} %copy-done.1, f32[18,432]{1,0:T(8,128)S(1)} %copy-done.2, f32[9,288]{1,0:T(8,128)S(1)} %copy-done.3), custom_call_target="tpu_custom_call" | custom-call | tf_op jit(solution)/shard_map/pallas_call | solution.py:597
Async XLA Ops:
  108.7 1.3 %copy-start = (bf16[1,2,256,1152]{3,2,1,0:T(8,128)(2,1)S(1)}, bf16[1,2,256,1152]{3,2,1,0:T(8,128)(2,1)}, u32[]{:S(2)}) copy-start(bf16[1,2,256,1152]{3,2,1,0:T(8,128)(2,1)} %get-tuple-element.12.refs_0_) | copy-start | bytes 3538948
  110.0 0.9 copy-start.1
  110.9 0.8 copy-start.2
  111.7 0.7 copy-start.3

commit v3 on v2

--- a/solution.py
+++ b/solution.py
@@ -28,10 +28,10 @@
 EPS = 1e-06
 VMEM_BYTES = 56 * 1024 * 1024
 
-PIECES = ((0, 0, 512), (0, 512, 384), (1, 0, 256), (1, 256, 384))
-FIRST_PIECES = ((0, 2), (1, 3))
+PIECES = ((0, 256), (256, 256), (512, 384))
+FIRST_PIECES = ((0, 1), (2,))
 BLOCK_Q = 144
-BLOCK_O = SLOT_E
+PACKED = 512
 OFFSETS = (4, 3, 5, 2, 6, 1, 7, 0)
 STEPS = 4
 HALF_ROWS = 256
@@ -84,11 +84,11 @@
 def fused_kernel(
     tok_in, dout_in, mod, wq, wo, tok_out, d_mod, oq, oo,
     tok, dout, m_send, d_send, m_all, d_all, wq_all, wo_all,
-    qkv, datt, att, att_slots, dbranch, dqkv, turned, d_in, gq, go,
-    back, xq, xo, sq, so, rq, ro, stage, final, part, parts, mods,
+    qkv, datt, att, dbranch, dqkv, turned, d_in, gq, go,
+    back, xq, xo, sq, rq, stage, final, stage_o, final_o, spread_o, last_o, part, parts, mods,
     here, a_send, a_recv, own_send, own_recv, w_send, w_recv, v_send, v_recv, t_send, t_recv,
     b_send, b_recv, x_send, x_recv, c_send, c_recv, p_send, p_recv,
-    z_send, z_recv, f_send, f_recv,
+    z_send, z_recv, f_send, f_recv, y_send, y_recv, o_send, o_recv, l_send, l_recv,
 ):
     seq, dp, clip, spot, half, core = place()
     twin = {"seq": seq, "dp": half * 2 + 1 - core}
@@ -128,7 +128,6 @@
         @pl.when(jnp.logical_or(half != core, h != half))
         def _():
             signal_all(barrier, [source(0, h)])
-    pl.semaphore_wait(barrier, jnp.where(half == core, 31, 32))
 
     shards, wholes = (wq, wo), (wq_all, wo_all)
 
@@ -173,10 +172,6 @@
             for n in range(2):
                 across_copy(n, parity, i).start()
 
-    by_parity(clip, send_across)
-    for n in range(2):
-        keep_copy(n).start()
-        own_copy(n).start()
     zeros = jnp.zeros((HALF_Q - 2 * SHARD_Q, WIDTH), BF16)
     wq_all[2 * SHARD_Q:HALF_Q, :] = zeros
     wq_all[HALF_Q + 2 * SHARD_Q:, :] = zeros
@@ -207,21 +202,46 @@
             for i, (src, dst) in enumerate(((m_send, m_all), (d_send, d_all)))
         ]
 
+    for n in range(2):
+        keep_copy(n).start()
     for copy in loads:
         copy.wait()
+
+    def prepare(part, d):
+        m_send[part, d], d_send[part, d] = blocks(part, d)
+
+    def prepare_step(part):
+        def step(d, carry):
+            prepare(part, d)
+            return carry
+
+        return step
+
+    lax.fori_loop(0, 8, prepare_step(0), 0, unroll=2)
+    pl.semaphore_wait(barrier, jnp.where(half == core, 31, 32))
+    by_parity(clip, send_across)
+
+    @pl.loop(1, 8)
+    def _(d):
+        for copy in spread_copies(0, d):
+            copy.start()
+
+    for n in range(2):
+        own_copy(n).start()
+
+    @pl.loop(1, 8)
+    def _(d):
+        prepare(1, d)
+        for copy in spread_copies(1, d):
+            copy.start()
+
+    prepare(1, 0)
     for part_ in range(2):
-        @pl.loop(1, 8)
-        def _(d):
-            m_send[part_, d], d_send[part_, d] = blocks(part_, d)
-            for copy in spread_copies(part_, d):
-                copy.start()
-
         at = slice(2 * part_, 2 * part_ + 2)
-        m_all[at, mine, :], d_all[at, mine, :] = blocks(part_, 0)
-
-    for ref, start in ((dqkv, 2 * SHARD_Q), (dqkv, HALF_Q + 2 * SHARD_Q)):
-        ref[:, start:start + 32] = jnp.zeros((ROWS, 32), BF16)
-    att_slots[...] = jnp.zeros_like(att_slots)
+        m_all[at, mine, :], d_all[at, mine, :] = m_send[part_, 0], d_send[part_, 0]
+
+    for start in (2 * SHARD_Q, HALF_Q + 2 * SHARD_Q):
+        dqkv[:, start:start + 32] = jnp.zeros((ROWS, 32), BF16)
 
     for i in range(4):
         def hand_on(parity):
@@ -279,7 +299,6 @@
         d_v = [dot(probs_b[h], da[h], (1, 0)).astype(BF16) for h in range(HEADS)]
         for h in range(HEADS):
             att[at, h * HD:h * HD + HD] = attended[h]
-            att_slots[at, h * SLOT_E:h * SLOT_E + HD] = attended[h]
             for part, grad in enumerate((d_q, d_k, d_v)):
                 dqkv[at, cols[h][part]:cols[h][part] + HD] = grad[h]
 
@@ -315,67 +334,113 @@
     def block(size, z):
         return pl.ds(pl.multiple_of(z * size, 16), size)
 
-    sizes = (BLOCK_Q, BLOCK_O)
-    terms, theirs = (gq, go), (xq, xo)
-
-    def pair_copy(i, n):
-        at = block(sizes[n], lax.rem(clip + OFFSETS[i], 8))
-        return remote(
-            terms[n].at[1 - core, at, :], theirs[n].at[at, :], x_send.at[i, n], x_recv.at[i, n], twin
-        )
-
-    turned[...] = m_all[...].reshape(ROWS, WIDTH).T
-    slots = att_slots[...].T
-
-    def weight_terms(h):
+    def pair_copy(i):
+        at = block(BLOCK_Q, lax.rem(clip + OFFSETS[i], 8))
+        return remote(gq.at[1 - core, at, :], xq.at[at, :], x_send.at[i], x_recv.at[i], twin)
+
+    def pair_copy_o():
+        return remote(go.at[1 - core], xo, y_send, y_recv, twin)
+
+    slot = lax.broadcasted_iota(jnp.int32, (HEADS * SLOT_E, HEADS * HD), 0)
+    inner = lax.rem(slot, SLOT_E)
+    from_ = lax.div(inner, 9) * HD + lax.div(slot, SLOT_E) * 9 + lax.rem(inner, 9)
+    pick = jnp.logical_and(
+        lax.broadcasted_iota(jnp.int32, (HEADS * SLOT_E, HEADS * HD), 1) == from_, inner < HD
+    )
+    slots = dot(pick.astype(F32).astype(BF16), att[...], (1, 1)).astype(BF16)
+
+    def out_terms(h):
         go[h] = dot(slots, dbranch[:, pl.ds(pl.multiple_of(h * START_O, 128), HALF_O)], (1, 0)).astype(BF16)
+
+    def qkv_terms(h):
         for first, lanes in ((0, 512), (512, 384)):
             src = pl.ds(pl.multiple_of(h * HALF_Q + first, 128), lanes)
             gq[h, :, first:first + lanes] = dot(turned[...], dqkv[:, src], (1, 0)).astype(BF16)
 
-    weight_terms(1 - core)
+    def plane_sends(copy, keep):
+        for d in range(1, 8):
+            for low in range(2):
+                copy(d, low).start()
+        for low in range(2):
+            is_self = jnp.logical_and(core == half, core == low)
+
+            @pl.when(is_self)
+            def _():
+                keep(low).start()
+
+            @pl.when(jnp.logical_not(is_self))
+            def _():
+                copy(0, low).start()
+
+    def plane_sent(copy):
+        for d in range(1, 8):
+            for low in range(2):
+                copy(d, low).wait_send()
+        for low in range(2):
+            @pl.when(jnp.logical_or(core != half, core != low))
+            def _():
+                copy(0, low).wait_send()
+
+    def plane_o(d, low):
+        to = half * 8 + d
+        return remote(
+            stage_o.at[lax.rem(spot + d, 8), :, 256 * low:256 * low + 384], final_o.at[to],
+            o_send.at[d, low], o_recv.at[to], owner(d, low),
+        )
+
+    def keep_o(low):
+        return pltpu.make_async_copy(
+            stage_o.at[spot, :, 256 * low:256 * low + 384], final_o.at[half * 8], o_recv.at[half * 8]
+        )
+
+    out_terms(1 - core)
+    pair_copy_o().start()
+    out_terms(core)
+    turned[...] = m_all[...].reshape(ROWS, WIDTH).T
+    qkv_terms(1 - core)
     for i in range(8):
-        for n in range(2):
-            pair_copy(i, n).start()
-    weight_terms(core)
-
-    def own(which, z, first, lanes):
-        at = block(sizes[which], z)
+        pair_copy(i).start()
+    pair_copy_o().wait_recv()
+    for j in range(8):
+        at = slice(SLOT_E * j, SLOT_E * j + SLOT_E)
+        stage_o[j] = (go[core, at, :].astype(F32) + xo[at, :].astype(F32)).astype(BF16)
+    plane_sends(plane_o, keep_o)
+    qkv_terms(core)
+
+    def own(z, first, lanes):
+        at = block(BLOCK_Q, z)
         return (
-            terms[which][core, at, first:first + lanes].astype(F32)
-            + theirs[which][at, first:first + lanes].astype(F32)
+            gq[core, at, first:first + lanes].astype(F32) + xq[at, first:first + lanes].astype(F32)
         )
 
     def pieces(k, way):
         return FIRST_PIECES[way] if k == 0 else range(len(PIECES))
 
     def chain_copy(way, k, n):
-        which, first, lanes = PIECES[n]
-        src, dst = ((sq, rq), (so, ro))[which]
+        first, lanes = PIECES[n]
         return remote(
-            src.at[way, k, :, first:first + lanes], dst.at[way, k, :, first:first + lanes],
+            sq.at[way, k, :, first:first + lanes], rq.at[way, k, :, first:first + lanes],
             c_send.at[way, k, n], c_recv.at[way, k, n], along(1 if way == 0 else 7),
         )
 
     def arrived(way, k, n):
-        which, first, lanes = PIECES[n]
+        first, lanes = PIECES[n]
         chain_copy(way, k, n).wait_recv()
-        return (rq, ro)[which][way, k, :, first:first + lanes].astype(F32)
+        return rq[way, k, :, first:first + lanes].astype(F32)
 
     def chain_step(k):
         for i in (0,) if k == 0 else (2 * k - 1, 2 * k):
-            for n in range(2):
-                pair_copy(i, n).wait_recv()
+            pair_copy(i).wait_recv()
         for n in range(len(PIECES)):
             for way in range(2):
                 if n not in pieces(k, way):
                     continue
-                which, first, lanes = PIECES[n]
+                first, lanes = PIECES[n]
                 z = lax.rem(clip + (4 - k if way == 0 else 4 + k), 8)
-                total = own(which, z, first, lanes)
+                total = own(z, first, lanes)
                 if k and n in pieces(k - 1, way):
                     total = total + arrived(way, k - 1, n)
-                (sq, so)[which][way, k, :, first:first + lanes] = total.astype(BF16)
+                sq[way, k, :, first:first + lanes] = total.astype(BF16)
                 chain_copy(way, k, n).start()
 
     chain_step(0)
@@ -386,8 +451,7 @@
         branch = dot(att[...], wo_all[lanes, :], (1, 1))
         grads = d_all[:, :, lanes].reshape(ROWS, 384).astype(F32)
         gates.append(jnp.sum(branch * grads, 0, keepdims=True))
-    part[2:3] = jnp.concatenate(gates, 1)
-    part[3:] = jnp.zeros((5, WIDTH), F32)
+    gate_row = jnp.concatenate(gates, 1)
 
     def tokens_back(half_):
         def step(d, carry):
@@ -419,13 +483,16 @@
         back[part_, 0] = d_in[2 * part_:2 * part_ + 2, mine, :]
         for d in range(1, 8):
             back_copy(part_, d).wait_recv()
-        sums = lax.fori_loop(0, 8, tokens_back(part_), sums)
+        sums = lax.fori_loop(0, 8, tokens_back(part_), sums, unroll=2)
         if part_ == 0:
             chain_step(1)
     result = pltpu.make_async_copy(dout, tok_out.at[0], here.at[4])
     result.start()
-    part[0:1] = jnp.sum(sums[0], 0, keepdims=True)
-    part[1:2] = jnp.sum(sums[1], 0, keepdims=True)
+    flat = jnp.concatenate(
+        [jnp.sum(sums[0], 0, keepdims=True), jnp.sum(sums[1], 0, keepdims=True), gate_row,
+         jnp.zeros((1, 8 * PACKED - 3 * WIDTH), F32)], 1
+    )
+    part[...] = jnp.concatenate([flat[:, PACKED * i:PACKED * i + PACKED] for i in range(8)], 0)
 
     def part_copy(d):
         return remote(part, parts.at[d], p_send.at[d], p_recv.at[d], peer(d))
@@ -433,31 +500,6 @@
     for d in range(1, 8):
         part_copy(d).start()
     chain_step(2)
-    total = part[...]
-    for d in range(1, 8):
-        part_copy(d).wait_recv()
-        total = total + parts[d]
-    mods[clip] = total
-
-    def mod_copy(d):
-        ref = mods.at[clip]
-        return remote(ref, ref, z_send.at[d], z_recv.at[d], along(d))
-
-    for d in range(1, 8):
-        mod_copy(d).start()
-    chain_step(3)
-    for n in range(2):
-        pair_copy(7, n).wait_recv()
-    sums_ = []
-    for which in range(2):
-        whole = []
-        for n, (which_n, first, lanes) in enumerate(PIECES):
-            if which_n == which:
-                total = own(which, clip, first, lanes)
-                for way in range(2):
-                    total = total + arrived(way, 3, n)
-                whole.append(total.astype(BF16))
-        sums_.append(jnp.concatenate(whole, 1))
 
     def widen(x, size, slot):
         count = 8 * slot
@@ -467,65 +509,90 @@
         pick = jnp.logical_and(col == lax.div(row, slot) * size + inside, inside < size)
         return dot(pick.astype(F32).astype(BF16), x, (1, 0)).astype(BF16)
 
-    wide_q, wide_o = widen(sums_[0], 18, 32), widen(sums_[1], 9, 16)
+    def plane_sum(ref, sems):
+        for i in range(16):
+            wait_bytes(ref.at[i], sems.at[i])
+        total = ref[0].astype(F32)
+        for i in range(1, 16):
+            total = total + ref[i].astype(F32)
+        return total
+
+    def last_copy(d):
+        return remote(
+            spread_o.at[lax.rem(clip + d, 8)], last_o.at[d], l_send.at[d], l_recv.at[d], along(d)
+        )
+
+    spread_o[...] = widen(plane_sum(final_o, o_recv).astype(BF16), 9, 16).reshape(8, 16, 384)
+    for d in range(1, 8):
+        last_copy(d).start()
+    total = part[...]
+    for d in range(1, 8):
+        part_copy(d).wait_recv()
+        total = total + parts[d]
+    mods[clip] = total
+
+    def mod_copy(d):
+        ref = mods.at[clip]
+        return remote(ref, ref, z_send.at[d], z_recv.at[d], along(d))
+
+    for d in range(1, 8):
+        mod_copy(d).start()
+    chain_step(3)
+    pair_copy(7).wait_recv()
+    whole = []
+    for n, (first, lanes) in enumerate(PIECES):
+        total = own(clip, first, lanes)
+        for way in range(2):
+            total = total + arrived(way, 3, n)
+        whole.append(total.astype(BF16))
+    wide = widen(jnp.concatenate(whole, 1), 18, 32)
     for j in range(8):
         for low in range(2):
-            stage[j, low, 0:32, :] = wide_q[32 * j:32 * j + 32, 384 * low:384 * low + 512]
-            stage[j, low, 32:48, 0:384] = wide_o[16 * j:16 * j + 16, 256 * low:256 * low + 384]
-            stage[j, low, 32:48, 384:512] = jnp.zeros((16, 128), BF16)
-
-    def owner_copy(d, low):
+            stage[j, low] = wide[32 * j:32 * j + 32, 384 * low:384 * low + 512]
+
+    def plane_q(d, low):
         to = half * 8 + d
-        return pltpu.make_async_remote_copy(
-            src_ref=stage.at[lax.rem(spot + d, 8), low], dst_ref=final.at[to],
-            send_sem=f_send.at[d, low], recv_sem=f_recv.at[to],
-            device_id=owner(d, low), device_id_type=MESH,
-        )
-
+        return remote(
+            stage.at[lax.rem(spot + d, 8), low], final.at[to],
+            f_send.at[d, low], f_recv.at[to], owner(d, low),
+        )
+
+    def keep_q(low):
+        return pltpu.make_async_copy(stage.at[spot, low], final.at[half * 8], f_recv.at[half * 8])
+
+    plane_sends(plane_q, keep_q)
+    total = spread_o[clip].astype(F32)
     for d in range(1, 8):
-        for low in range(2):
-            owner_copy(d, low).start()
-    for low in range(2):
-        is_self = jnp.logical_and(core == half, core == low)
-
-        @pl.when(is_self)
-        def _():
-            pltpu.make_async_copy(stage.at[spot, low], final.at[half * 8], f_recv.at[half * 8]).start()
-
-        @pl.when(jnp.logical_not(is_self))
-        def _():
-            owner_copy(0, low).start()
-
-    for i in range(16):
-        wait_bytes(final.at[i], f_recv.at[i])
-    total = final[0].astype(F32)
-    for i in range(1, 16):
-        total = total + final[i].astype(F32)
-    got_q = jnp.where(core == 0, total[0:32, 0:SHARD_Q], total[0:32, 48:48 + SHARD_Q])
+        last_copy(d).wait_recv()
+        total = total + last_o[d].astype(F32)
     first_o = 64 * half + 32 * core
-    got_o = total[32:48, 0:SHARD_O]
+    got_o = total[:, 0:SHARD_O]
     for start in (32, 64, 96):
-        got_o = jnp.where(first_o == start, total[32:48, start:start + SHARD_O], got_o)
-    oq[...] = got_q[0:18]
+        got_o = jnp.where(first_o == start, total[:, start:start + SHARD_O], got_o)
     oo[...] = got_o[0:9]
-
     for d in range(1, 8):
         mod_copy(d).wait()
+    flats = [jnp.concatenate([mods[z, i:i + 1] for i in range(8)], 1) for z in range(8)]
+    for i in range(3):
+        d_mod[0, i] = jnp.concatenate([flat[:, WIDTH * i:WIDTH * i + WIDTH] for flat in flats], 0)
+    total = plane_sum(final, f_recv)
+    got_q = jnp.where(core == 0, total[:, 0:SHARD_Q], total[:, 48:48 + SHARD_Q])
+    oq[...] = got_q[0:18]
+
+    plane_sent(plane_o)
+    plane_sent(plane_q)
+    for d in range(1, 8):
+        last_copy(d).wait_send()
         part_copy(d).wait_send()
         for part_ in range(2):
             back_copy(part_, d).wait_send()
             for copy in spread_copies(part_, d):
                 copy.wait_send()
-        for low in range(2):
-            owner_copy(d, low).wait_send()
-    for low in range(2):
-        @pl.when(jnp.logical_or(core != half, core != low))
-        def _():
-            owner_copy(0, low).wait_send()
+    pair_copy_o().wait_send()
     for n in range(2):
         own_copy(n).wait_send()
-        for i in range(8):
-            pair_copy(i, n).wait_send()
+    for i in range(8):
+        pair_copy(i).wait_send()
     for k in range(STEPS):
         for way in range(2):
             for n in pieces(k, way):
@@ -540,15 +607,18 @@
                 twin_copy(n, 1 - parity, i, 1).wait_send()
 
     by_parity(clip, sent)
-    for i in range(3):
-        d_mod[0, i] = jnp.concatenate([mods[z, i:i + 1] for z in range(8)], 0)
     result.wait()
 
 
 def copy_kernel(*refs):
-    count = len(refs) // 2
-    for i in range(count):
-        refs[count + i][...] = refs[i][...]
+    count = (len(refs) - 1) // 2
+    copies = [
+        pltpu.make_async_copy(refs[i], refs[count + i], refs[-1].at[i]) for i in range(count)
+    ]
+    for copy in copies:
+        copy.start()
+    for copy in copies:
+        copy.wait()
 
 
 def body(tokens, d_out, modulation, w_qkv, w_out):
@@ -577,18 +647,19 @@
             held(CHUNKS, CHUNK, WIDTH), held(CHUNKS, CHUNK, WIDTH),
             held(2 * HALF_Q, WIDTH), held(WIDTH, HEADS * HD),
             held(ROWS, 2 * HALF_Q), held(ROWS, HEADS * HD), held(ROWS, HEADS * HD),
-            held(ROWS, HEADS * SLOT_E), held(ROWS, WIDTH), held(ROWS, 2 * HALF_Q),
+            held(ROWS, WIDTH), held(ROWS, 2 * HALF_Q),
             held(WIDTH, ROWS), held(CHUNKS, CHUNK, WIDTH),
             held(2, WIDTH, HALF_Q), held(2, HEADS * SLOT_E, HALF_O),
             held(2, 8, 2, 16, WIDTH), held(WIDTH, HALF_Q), held(HEADS * SLOT_E, HALF_O),
-            held(2, STEPS, BLOCK_Q, HALF_Q), held(2, STEPS, BLOCK_O, HALF_O),
-            held(2, STEPS, BLOCK_Q, HALF_Q), held(2, STEPS, BLOCK_O, HALF_O),
-            held(8, 2, 48, 512), held(16, 48, 512),
-            held(8, WIDTH, dtype=F32), held(8, 8, WIDTH, dtype=F32), held(8, 8, WIDTH, dtype=F32),
+            held(2, STEPS, BLOCK_Q, HALF_Q), held(2, STEPS, BLOCK_Q, HALF_Q),
+            held(8, 2, 32, 512), held(16, 32, 512), held(8, SLOT_E, HALF_O), held(16, SLOT_E, 384),
+            held(8, 16, 384), held(8, 16, 384),
+            held(8, PACKED, dtype=F32), held(8, 8, PACKED, dtype=F32), held(8, 8, PACKED, dtype=F32),
             dma((5,)), dma((2, 2, 8)), dma((2, 2, 8)), dma((2,)), dma((2,)),
             dma((2, 4)), dma((2, 4)), dma((2, 4)), dma((2, 4)), dma((2, 4, 2)), dma((2, 4, 2)),
-            dma((2, 8)), dma((2, 8)), dma((8, 2)), dma((8, 2)), dma(chains), dma(chains),
+            dma((2, 8)), dma((2, 8)), dma((8,)), dma((8,)), dma(chains), dma(chains),
             dma((8,)), dma((8,)), dma((8,)), dma((8,)), dma((8, 2)), dma((16,)),
+            dma, dma, dma((8, 2)), dma((16,)), dma((8,)), dma((8,)),
         ],
         compiler_params=pltpu.CompilerParams(
             vmem_limit_bytes=VMEM_BYTES, collective_id=0, has_side_effects=True
@@ -597,9 +668,10 @@
     d_tokens, d_mod, g_qkv, g_out = pl.pallas_call(
         copy_kernel,
         out_shape=outs,
-        in_specs=[inside] * 4,
+        in_specs=[anywhere] * 4,
         out_specs=[inside] * 4,
-        compiler_params=pltpu.CompilerParams(vmem_limit_bytes=16 * 1024 * 1024),
+        scratch_shapes=[dma((4,))],
+        compiler_params=pltpu.CompilerParams(vmem_limit_bytes=VMEM_BYTES),
     )(*results)
     return d_tokens, jnp.swapaxes(d_mod, 1, 2), g_qkv.T, g_out.T
 

time: 114 us -> 102 us (0.89)
  Pallas kernels: 109 us -> 101 us
  local copies, waits for them, and re-layouts: 3.69 us -> 0 us
    pallas_call x1, Pallas kernels: 108 us -> 98.6 us  [body(): pl.pallas_call(fused_kernel, out_shape=outs, in_specs=[anywhere, anywhere...]
    unnamed x8 -> x0, local copies, waits for them, and re-layouts: 3.69 us -> none
    pallas_call x1, Pallas kernels: 1.15 us -> 2.37 us  [body(): pl.pallas_call(copy_kernel, out_shape=outs, in_specs=[anywhere] * 4, out_...]
where the time goes in v3:
time: 102 us
  Pallas kernels  101 us (99%)
    pallas_call x1, Pallas kernels, body(): pl.pallas_call(fused_kernel, out_shape=outs, in_specs=[anywhere, anywhere...  98.6 us
    pallas_call x1, Pallas kernels, body(): pl.pallas_call(copy_kernel, out_shape=outs, in_specs=[anywhere] * 4, out_...  2.37 us

profile of v3, /device:TPU:1, one launch (start us, length us, event | category | flops | bytes accessed | tf_op | source)
XLA Modules:
  0.0 101.8 jit_solution(10925044323532162874)
XLA Ops:
  0.6 98.6 %shard_map.84 = (bf16[1,2,256,1152]{3,2,1,0:T(8,128)(2,1)}, f32[1,3,8,1152]{3,2,1,0:T(8,128)}, f32[18,432]{1,0:T(8,128)}, f32[9,288]{1,0:T(8,128)}) custom-call(bf16[1,2,256,1152]{3,2,1,0:T(8,128)(2,1)} %tok_in.1, bf16[1,2,256,1152]{3,2,1,0:T(8,128)(2,1)} %dout_in.1, f32[1,3,8,1152]{3,2,1,0:T(8,128)} %bitcast.4, bf16[432,1152]{1,0:T(8,128)(2,1)} %wq.1, ...), custom_call_target="tpu_custom_call" | custom-call | tf_op jit(solution)/shard_map/pallas_call | solution.py:639
  99.2 2.4 %shard_map.85 = (bf16[1,2,256,1152]{3,2,1,0:T(8,128)(2,1)}, f32[1,3,8,1152]{3,2,1,0:T(8,128)}, f32[18,432]{1,0:T(8,128)}, f32[9,288]{1,0:T(8,128)}) custom-call(bf16[1,2,256,1152]{3,2,1,0:T(8,128)(2,1)} %get-tuple-element.12.refs_0_, f32[1,3,8,1152]{3,2,1,0:T(8,128)} %get-tuple-element.13.refs_1_, f32[18,432]{1,0:T(8,128)} %get-tuple-element.14.refs_2_, ...), custom_call_target="tpu_custom_call" | custom-call | tf_op jit(solution)/shard_map/pallas_call | solution.py:668

commit v4 on v3

--- a/solution.py
+++ b/solution.py
@@ -28,10 +28,16 @@
 EPS = 1e-06
 VMEM_BYTES = 56 * 1024 * 1024
 
-PIECES = ((0, 256), (256, 256), (512, 384))
-FIRST_PIECES = ((0, 1), (2,))
+PIECES = ((0, 256), (256, 256), (512, 256))
+FIRST_PIECES = ((0,), (1, 2))
+CHAIN_LANES = 768
+PLANE_LANES = 128
+FINAL_LANES = 512
+HIGH_LANES = CHAIN_LANES - 384
+HIGH_FIRST = HIGH_LANES - 48
 BLOCK_Q = 144
 PACKED = 512
+
 OFFSETS = (4, 3, 5, 2, 6, 1, 7, 0)
 STEPS = 4
 HALF_ROWS = 256
@@ -84,11 +90,12 @@
 def fused_kernel(
     tok_in, dout_in, mod, wq, wo, tok_out, d_mod, oq, oo,
     tok, dout, m_send, d_send, m_all, d_all, wq_all, wo_all,
-    qkv, datt, att, dbranch, dqkv, turned, d_in, gq, go,
-    back, xq, xo, sq, rq, stage, final, stage_o, final_o, spread_o, last_o, part, parts, mods,
+    qkv, datt, att, dbranch, dqkv, turned, turned_p, perm, d_in, gq, gp, go,
+    back, xq, xp, xo, sq, rq, stage, final, stage_p, final_p, spread_p, last_p, stage_o, final_o, spread_o, last_o, part, parts, mods,
     here, a_send, a_recv, own_send, own_recv, w_send, w_recv, v_send, v_recv, t_send, t_recv,
     b_send, b_recv, x_send, x_recv, c_send, c_recv, p_send, p_recv,
     z_send, z_recv, f_send, f_recv, y_send, y_recv, o_send, o_recv, l_send, l_recv,
+    yp_send, yp_recv, op_send, op_recv, lp_send, lp_recv,
 ):
     seq, dp, clip, spot, half, core = place()
     twin = {"seq": seq, "dp": half * 2 + 1 - core}
@@ -193,14 +200,17 @@
         normed, _ = normalise(tok[:, at, :].astype(F32))
         return arranged(normed * scale + shift), arranged(dout[:, at, :].astype(F32))
 
-    def spread_copies(part, d):
-        return [
-            remote(
-                src.at[part, d], dst.at[2 * part:2 * part + 2, mine, :],
-                a_send.at[i, part, d], a_recv.at[i, part, d], peer(d),
-            )
-            for i, (src, dst) in enumerate(((m_send, m_all), (d_send, d_all)))
-        ]
+    def spread_copy(i, part, d):
+        src, dst = ((m_send, m_all), (d_send, d_all))[i]
+        return remote(
+            src.at[part, d], dst.at[2 * part:2 * part + 2, mine, :],
+            a_send.at[i, part, d], a_recv.at[i, part, d], peer(d),
+        )
+
+    def spread(i, part):
+        @pl.loop(1, 8)
+        def _(d):
+            spread_copy(i, part, d).start()
 
     for n in range(2):
         keep_copy(n).start()
@@ -221,19 +231,15 @@
     pl.semaphore_wait(barrier, jnp.where(half == core, 31, 32))
     by_parity(clip, send_across)
 
-    @pl.loop(1, 8)
-    def _(d):
-        for copy in spread_copies(0, d):
-            copy.start()
-
+    spread(0, 0)
+    spread(1, 0)
     for n in range(2):
         own_copy(n).start()
 
     @pl.loop(1, 8)
     def _(d):
         prepare(1, d)
-        for copy in spread_copies(1, d):
-            copy.start()
+        spread_copy(0, 1, d).start()
 
     prepare(1, 0)
     for part_ in range(2):
@@ -251,6 +257,16 @@
                 twin_copy(n, parity, i, 0).start()
 
         by_parity(clip, hand_on)
+        if i == 1:
+            spread(1, 1)
+    @pl.loop(0, 9)
+    def _(n):
+        row = lax.broadcasted_iota(jnp.int32, (128, 1), 0) + n * 128
+        inner = lax.rem(row, BLOCK_Q)
+        from_ = lax.div(inner, 18) * BLOCK_Q + lax.div(row, BLOCK_Q) * 18 + lax.rem(inner, 18)
+        found = lax.broadcasted_iota(jnp.int32, (128, WIDTH), 1) == from_
+        perm[pl.ds(pl.multiple_of(n * 128, 128), 128), :] = found.astype(F32).astype(BF16)
+
     for i in range(4):
         def hand_twin(parity):
             for n in range(2):
@@ -310,13 +326,17 @@
         )
 
     for part_ in range(2):
-        for d in range(1, 8):
-            for copy in spread_copies(part_, d):
-                copy.wait_recv()
         two = slice(2 * part_, 2 * part_ + 2)
         at = slice(part_ * HALF_ROWS, part_ * HALF_ROWS + HALF_ROWS)
+        for d in range(1, 8):
+            spread_copy(0, part_, d).wait_recv()
         m = m_all[two].reshape(HALF_ROWS, WIDTH)
         qkv[at, :] = dot(m, wq_all[...], (1, 1)).astype(BF16)
+        if part_ == 0:
+            turned[:, at] = m.T
+            turned_p[:, at] = dot(perm[...], m, (1, 1)).astype(BF16)
+        for d in range(1, 8):
+            spread_copy(1, part_, d).wait_recv()
         dbranch[at, :] = (gate * d_all[two].reshape(HALF_ROWS, WIDTH).astype(F32)).astype(BF16)
         datt[at, :] = dot(dbranch[at, :], wo_all[...], (1, 0)).astype(BF16)
 
@@ -352,10 +372,16 @@
     def out_terms(h):
         go[h] = dot(slots, dbranch[:, pl.ds(pl.multiple_of(h * START_O, 128), HALF_O)], (1, 0)).astype(BF16)
 
-    def qkv_terms(h):
-        for first, lanes in ((0, 512), (512, 384)):
-            src = pl.ds(pl.multiple_of(h * HALF_Q + first, 128), lanes)
-            gq[h, :, first:first + lanes] = dot(turned[...], dqkv[:, src], (1, 0)).astype(BF16)
+    def pair_copy_p():
+        return remote(gp.at[1 - core], xp, yp_send, yp_recv, twin)
+
+    def chain_terms(h):
+        src = pl.ds(pl.multiple_of(h * HALF_Q, 128), CHAIN_LANES)
+        gq[h] = dot(turned[...], dqkv[:, src], (1, 0)).astype(BF16)
+
+    def plane_terms(h):
+        src = pl.ds(pl.multiple_of(h * HALF_Q + CHAIN_LANES, 128), PLANE_LANES)
+        gp[h] = dot(turned_p[...], dqkv[:, src], (1, 0)).astype(BF16)
 
     def plane_sends(copy, keep):
         for d in range(1, 8):
@@ -393,19 +419,18 @@
             stage_o.at[spot, :, 256 * low:256 * low + 384], final_o.at[half * 8], o_recv.at[half * 8]
         )
 
-    out_terms(1 - core)
-    pair_copy_o().start()
-    out_terms(core)
-    turned[...] = m_all[...].reshape(ROWS, WIDTH).T
-    qkv_terms(1 - core)
+    def plane_p(d):
+        to = half * 8 + d
+        return remote(
+            stage_p.at[lax.rem(spot + d, 8)], final_p.at[to], op_send.at[d], op_recv.at[to], owner(d, 1)
+        )
+
+    late = m_all[2:4].reshape(HALF_ROWS, WIDTH)
+    turned[:, HALF_ROWS:] = late.T
+    chain_terms(1 - core)
     for i in range(8):
         pair_copy(i).start()
-    pair_copy_o().wait_recv()
-    for j in range(8):
-        at = slice(SLOT_E * j, SLOT_E * j + SLOT_E)
-        stage_o[j] = (go[core, at, :].astype(F32) + xo[at, :].astype(F32)).astype(BF16)
-    plane_sends(plane_o, keep_o)
-    qkv_terms(core)
+    chain_terms(core)
 
     def own(z, first, lanes):
         at = block(BLOCK_Q, z)
@@ -444,6 +469,35 @@
                 chain_copy(way, k, n).start()
 
     chain_step(0)
+    turned_p[:, HALF_ROWS:] = dot(perm[...], late, (1, 1)).astype(BF16)
+    plane_terms(1 - core)
+    pair_copy_p().start()
+    out_terms(1 - core)
+    pair_copy_o().start()
+    plane_terms(core)
+    out_terms(core)
+    chain_step(1)
+    pair_copy_o().wait_recv()
+    for j in range(8):
+        at = slice(SLOT_E * j, SLOT_E * j + SLOT_E)
+        stage_o[j] = (go[core, at, :].astype(F32) + xo[at, :].astype(F32)).astype(BF16)
+    plane_sends(plane_o, keep_o)
+
+    pair_copy_p().wait_recv()
+    for j in range(8):
+        at = slice(BLOCK_Q * j, BLOCK_Q * j + BLOCK_Q)
+        stage_p[j] = (gp[core, at, :].astype(F32) + xp[at, :].astype(F32)).astype(BF16)
+    for d in range(1, 8):
+        plane_p(d).start()
+    own_p = jnp.logical_and(core == half, core == 1)
+
+    @pl.when(own_p)
+    def _():
+        pltpu.make_async_copy(stage_p.at[spot], final_p.at[half * 8], op_recv.at[half * 8]).start()
+
+    @pl.when(jnp.logical_not(own_p))
+    def _():
+        plane_p(0).start()
 
     gates = []
     for n in range(3):
@@ -477,6 +531,7 @@
 
         return step
 
+    chain_step(2)
     zero = jnp.zeros((8, WIDTH), F32)
     sums = (zero, zero)
     for part_ in range(2):
@@ -485,7 +540,7 @@
             back_copy(part_, d).wait_recv()
         sums = lax.fori_loop(0, 8, tokens_back(part_), sums, unroll=2)
         if part_ == 0:
-            chain_step(1)
+            chain_step(3)
     result = pltpu.make_async_copy(dout, tok_out.at[0], here.at[4])
     result.start()
     flat = jnp.concatenate(
@@ -499,7 +554,6 @@
 
     for d in range(1, 8):
         part_copy(d).start()
-    chain_step(2)
 
     def widen(x, size, slot):
         count = 8 * slot
@@ -509,35 +563,6 @@
         pick = jnp.logical_and(col == lax.div(row, slot) * size + inside, inside < size)
         return dot(pick.astype(F32).astype(BF16), x, (1, 0)).astype(BF16)
 
-    def plane_sum(ref, sems):
-        for i in range(16):
-            wait_bytes(ref.at[i], sems.at[i])
-        total = ref[0].astype(F32)
-        for i in range(1, 16):
-            total = total + ref[i].astype(F32)
-        return total
-
-    def last_copy(d):
-        return remote(
-            spread_o.at[lax.rem(clip + d, 8)], last_o.at[d], l_send.at[d], l_recv.at[d], along(d)
-        )
-
-    spread_o[...] = widen(plane_sum(final_o, o_recv).astype(BF16), 9, 16).reshape(8, 16, 384)
-    for d in range(1, 8):
-        last_copy(d).start()
-    total = part[...]
-    for d in range(1, 8):
-        part_copy(d).wait_recv()
-        total = total + parts[d]
-    mods[clip] = total
-
-    def mod_copy(d):
-        ref = mods.at[clip]
-        return remote(ref, ref, z_send.at[d], z_recv.at[d], along(d))
-
-    for d in range(1, 8):
-        mod_copy(d).start()
-    chain_step(3)
     pair_copy(7).wait_recv()
     whole = []
     for n, (first, lanes) in enumerate(PIECES):
@@ -546,21 +571,66 @@
             total = total + arrived(way, 3, n)
         whole.append(total.astype(BF16))
     wide = widen(jnp.concatenate(whole, 1), 18, 32)
-    for j in range(8):
-        for low in range(2):
-            stage[j, low] = wide[32 * j:32 * j + 32, 384 * low:384 * low + 512]
+    stage[...] = wide.reshape(8, 32, CHAIN_LANES)
+
+    def from_stage(j, low):
+        return stage.at[j, :, 0:FINAL_LANES] if low == 0 else stage.at[j, :, 384:CHAIN_LANES]
+
+    def to_final(i, low):
+        return final.at[i] if low == 0 else final.at[i, :, 0:HIGH_LANES]
 
     def plane_q(d, low):
         to = half * 8 + d
         return remote(
-            stage.at[lax.rem(spot + d, 8), low], final.at[to],
+            from_stage(lax.rem(spot + d, 8), low), to_final(to, low),
             f_send.at[d, low], f_recv.at[to], owner(d, low),
         )
 
     def keep_q(low):
-        return pltpu.make_async_copy(stage.at[spot, low], final.at[half * 8], f_recv.at[half * 8])
+        return pltpu.make_async_copy(from_stage(spot, low), to_final(half * 8, low), f_recv.at[half * 8])
 
     plane_sends(plane_q, keep_q)
+
+    total = part[...]
+    for d in range(1, 8):
+        part_copy(d).wait_recv()
+        total = total + parts[d]
+    mods[clip] = total
+
+    def mod_copy(d):
+        ref = mods.at[clip]
+        return remote(ref, ref, z_send.at[d], z_recv.at[d], along(d))
+
+    for d in range(1, 8):
+        mod_copy(d).start()
+
+    def plane_sum(ref, sems):
+        for i in range(16):
+            wait_bytes(ref.at[i], sems.at[i])
+        total = ref[0].astype(F32)
+        for i in range(1, 16):
+            total = total + ref[i].astype(F32)
+        return total
+
+    def last_copy(d):
+        return remote(
+            spread_o.at[lax.rem(clip + d, 8)], last_o.at[d], l_send.at[d], l_recv.at[d], along(d)
+        )
+
+    spread_o[...] = widen(plane_sum(final_o, o_recv).astype(BF16), 9, 16).reshape(8, 16, 384)
+    for d in range(1, 8):
+        last_copy(d).start()
+    def last_copy_p(d):
+        return remote(
+            spread_p.at[lax.rem(clip + d, 8)], last_p.at[d], lp_send.at[d], lp_recv.at[d], along(d)
+        )
+
+    @pl.when(core == 1)
+    def _():
+        spread_p[...] = widen(plane_sum(final_p, op_recv).astype(BF16), 18, 32).reshape(8, 32, PLANE_LANES)
+        for d in range(1, 8):
+            last_copy_p(d).start()
+
     total = spread_o[clip].astype(F32)
     for d in range(1, 8):
         last_copy(d).wait_recv()
@@ -575,10 +645,33 @@
     flats = [jnp.concatenate([mods[z, i:i + 1] for i in range(8)], 1) for z in range(8)]
     for i in range(3):
         d_mod[0, i] = jnp.concatenate([flat[:, WIDTH * i:WIDTH * i + WIDTH] for flat in flats], 0)
-    total = plane_sum(final, f_recv)
-    got_q = jnp.where(core == 0, total[:, 0:SHARD_Q], total[:, 48:48 + SHARD_Q])
-    oq[...] = got_q[0:18]
-
+    @pl.when(core == 0)
+    def _():
+        oq[...] = plane_sum(final, f_recv)[0:18, 0:SHARD_Q]
+
+    @pl.when(core == 1)
+    def _():
+        rest = spread_p[clip].astype(F32)
+        for d in range(1, 8):
+            last_copy_p(d).wait_recv()
+            rest = rest + last_p[d].astype(F32)
+        for i in range(16):
+            wait_bytes(to_final(i, 1), f_recv.at[i])
+        first = final[0, :, 0:HIGH_LANES].astype(F32)
+        for i in range(1, 16):
+            first = first + final[i, :, 0:HIGH_LANES].astype(F32)
+        oq[...] = jnp.concatenate([first[0:18, 48:HIGH_LANES], rest[0:18, 0:SHARD_Q - HIGH_FIRST]], 1)
+        for d in range(1, 8):
+            last_copy_p(d).wait_send()
+
+    for d in range(1, 8):
+        plane_p(d).wait_send()
+
+    @pl.when(jnp.logical_not(own_p))
+    def _():
+        plane_p(0).wait_send()
+
+    pair_copy_p().wait_send()
     plane_sent(plane_o)
     plane_sent(plane_q)
     for d in range(1, 8):
@@ -586,8 +679,8 @@
         part_copy(d).wait_send()
         for part_ in range(2):
             back_copy(part_, d).wait_send()
-            for copy in spread_copies(part_, d):
-                copy.wait_send()
+            for i in range(2):
+                spread_copy(i, part_, d).wait_send()
     pair_copy_o().wait_send()
     for n in range(2):
         own_copy(n).wait_send()
@@ -648,11 +741,15 @@
             held(2 * HALF_Q, WIDTH), held(WIDTH, HEADS * HD),
             held(ROWS, 2 * HALF_Q), held(ROWS, HEADS * HD), held(ROWS, HEADS * HD),
             held(ROWS, WIDTH), held(ROWS, 2 * HALF_Q),
-            held(WIDTH, ROWS), held(CHUNKS, CHUNK, WIDTH),
-            held(2, WIDTH, HALF_Q), held(2, HEADS * SLOT_E, HALF_O),
-            held(2, 8, 2, 16, WIDTH), held(WIDTH, HALF_Q), held(HEADS * SLOT_E, HALF_O),
-            held(2, STEPS, BLOCK_Q, HALF_Q), held(2, STEPS, BLOCK_Q, HALF_Q),
-            held(8, 2, 32, 512), held(16, 32, 512), held(8, SLOT_E, HALF_O), held(16, SLOT_E, 384),
+            held(WIDTH, ROWS), held(WIDTH, ROWS), held(WIDTH, WIDTH), held(CHUNKS, CHUNK, WIDTH),
+            held(2, WIDTH, CHAIN_LANES), held(2, WIDTH, PLANE_LANES), held(2, HEADS * SLOT_E, HALF_O),
+            held(2, 8, 2, 16, WIDTH),
+            held(WIDTH, CHAIN_LANES), held(WIDTH, PLANE_LANES), held(HEADS * SLOT_E, HALF_O),
+            held(2, STEPS, BLOCK_Q, CHAIN_LANES), held(2, STEPS, BLOCK_Q, CHAIN_LANES),
+            held(8, 32, CHAIN_LANES), held(16, 32, FINAL_LANES),
+            held(8, BLOCK_Q, PLANE_LANES), held(16, BLOCK_Q, PLANE_LANES),
+            held(8, 32, PLANE_LANES), held(8, 32, PLANE_LANES),
+            held(8, SLOT_E, HALF_O), held(16, SLOT_E, 384),
             held(8, 16, 384), held(8, 16, 384),
             held(8, PACKED, dtype=F32), held(8, 8, PACKED, dtype=F32), held(8, 8, PACKED, dtype=F32),
             dma((5,)), dma((2, 2, 8)), dma((2, 2, 8)), dma((2,)), dma((2,)),
@@ -660,6 +757,7 @@
             dma((2, 8)), dma((2, 8)), dma((8,)), dma((8,)), dma(chains), dma(chains),
             dma((8,)), dma((8,)), dma((8,)), dma((8,)), dma((8, 2)), dma((16,)),
             dma, dma, dma((8, 2)), dma((16,)), dma((8,)), dma((8,)),
+            dma, dma, dma((8,)), dma((16,)), dma((8,)), dma((8,)),
         ],
         compiler_params=pltpu.CompilerParams(
             vmem_limit_bytes=VMEM_BYTES, collective_id=0, has_side_effects=True

time: 102 us -> 94.8 us (0.929)
  Pallas kernels: 101 us -> 93.8 us
    pallas_call x1, Pallas kernels: 98.6 us -> 91.5 us  [body(): pl.pallas_call(fused_kernel, out_shape=outs, in_specs=[anywhere, anywhere...]
where the time goes in v4:
time: 94.8 us; the launch traced here: 94.6 us
  Pallas kernels  93.8 us (99%)
    pallas_call x1, Pallas kernels, body(): pl.pallas_call(fused_kernel, out_shape=outs, in_specs=[anywhere, anywhere...  91.5 us
    pallas_call x1, Pallas kernels, body(): pl.pallas_call(copy_kernel, out_shape=outs, in_specs=[anywhere] * 4, out_...  2.37 us

profile of v4, /device:TPU:1, one launch (start us, length us, event | category | flops | bytes accessed | tf_op | source)
XLA Modules:
  0.0 94.6 jit_solution(5263803001817496703)
XLA Ops:
  0.6 91.5 %shard_map.84 = (bf16[1,2,256,1152]{3,2,1,0:T(8,128)(2,1)}, f32[1,3,8,1152]{3,2,1,0:T(8,128)}, f32[18,432]{1,0:T(8,128)}, f32[9,288]{1,0:T(8,128)}) custom-call(bf16[1,2,256,1152]{3,2,1,0:T(8,128)(2,1)} %tok_in.1, bf16[1,2,256,1152]{3,2,1,0:T(8,128)(2,1)} %dout_in.1, f32[1,3,8,1152]{3,2,1,0:T(8,128)} %bitcast.4, bf16[432,1152]{1,0:T(8,128)(2,1)} %wq.1, ...), custom_call_target="tpu_custom_call" | custom-call | tf_op jit(solution)/shard_map/pallas_call | solution.py:732
  92.1 2.4 %shard_map.85 = (bf16[1,2,256,1152]{3,2,1,0:T(8,128)(2,1)}, f32[1,3,8,1152]{3,2,1,0:T(8,128)}, f32[18,432]{1,0:T(8,128)}, f32[9,288]{1,0:T(8,128)}) custom-call(bf16[1,2,256,1152]{3,2,1,0:T(8,128)(2,1)} %get-tuple-element.12.refs_0_, f32[1,3,8,1152]{3,2,1,0:T(8,128)} %get-tuple-element.13.refs_1_, f32[18,432]{1,0:T(8,128)} %get-tuple-element.14.refs_2_, ...), custom_call_target="tpu_custom_call" | custom-call | tf_op jit(solution)/shard_map/pallas_call | solution.py:766

commit v5 on v4

--- a/solution.py
+++ b/solution.py
@@ -28,13 +28,10 @@
 EPS = 1e-06
 VMEM_BYTES = 56 * 1024 * 1024
 
-PIECES = ((0, 256), (256, 256), (512, 256))
-FIRST_PIECES = ((0,), (1, 2))
-CHAIN_LANES = 768
-PLANE_LANES = 128
+PIECES = ((0, 256), (256, 256), (512, 384))
+FIRST_PIECES = ((0, 1), (2,))
+CHAIN_LANES = 896
 FINAL_LANES = 512
-HIGH_LANES = CHAIN_LANES - 384
-HIGH_FIRST = HIGH_LANES - 48
 BLOCK_Q = 144
 PACKED = 512
 
@@ -90,12 +87,11 @@
 def fused_kernel(
     tok_in, dout_in, mod, wq, wo, tok_out, d_mod, oq, oo,
     tok, dout, m_send, d_send, m_all, d_all, wq_all, wo_all,
-    qkv, datt, att, dbranch, dqkv, turned, turned_p, perm, d_in, gq, gp, go,
-    back, xq, xp, xo, sq, rq, stage, final, stage_p, final_p, spread_p, last_p, stage_o, final_o, spread_o, last_o, part, parts, mods,
+    qkv, datt, att, dbranch, dqkv, turned, d_in, gq, go,
+    back, xq, xo, sq, rq, stage, final, stage_o, final_o, spread_o, last_o, part, parts, mods,
     here, a_send, a_recv, own_send, own_recv, w_send, w_recv, v_send, v_recv, t_send, t_recv,
     b_send, b_recv, x_send, x_recv, c_send, c_recv, p_send, p_recv,
     z_send, z_recv, f_send, f_recv, y_send, y_recv, o_send, o_recv, l_send, l_recv,
-    yp_send, yp_recv, op_send, op_recv, lp_send, lp_recv,
 ):
     seq, dp, clip, spot, half, core = place()
     twin = {"seq": seq, "dp": half * 2 + 1 - core}
@@ -259,14 +255,6 @@
         by_parity(clip, hand_on)
         if i == 1:
             spread(1, 1)
-    @pl.loop(0, 9)
-    def _(n):
-        row = lax.broadcasted_iota(jnp.int32, (128, 1), 0) + n * 128
-        inner = lax.rem(row, BLOCK_Q)
-        from_ = lax.div(inner, 18) * BLOCK_Q + lax.div(row, BLOCK_Q) * 18 + lax.rem(inner, 18)
-        found = lax.broadcasted_iota(jnp.int32, (128, WIDTH), 1) == from_
-        perm[pl.ds(pl.multiple_of(n * 128, 128), 128), :] = found.astype(F32).astype(BF16)
-
     for i in range(4):
         def hand_twin(parity):
             for n in range(2):
@@ -334,7 +322,6 @@
         qkv[at, :] = dot(m, wq_all[...], (1, 1)).astype(BF16)
         if part_ == 0:
             turned[:, at] = m.T
-            turned_p[:, at] = dot(perm[...], m, (1, 1)).astype(BF16)
         for d in range(1, 8):
             spread_copy(1, part_, d).wait_recv()
         dbranch[at, :] = (gate * d_all[two].reshape(HALF_ROWS, WIDTH).astype(F32)).astype(BF16)
@@ -372,16 +359,9 @@
     def out_terms(h):
         go[h] = dot(slots, dbranch[:, pl.ds(pl.multiple_of(h * START_O, 128), HALF_O)], (1, 0)).astype(BF16)
 
-    def pair_copy_p():
-        return remote(gp.at[1 - core], xp, yp_send, yp_recv, twin)
-
     def chain_terms(h):
         src = pl.ds(pl.multiple_of(h * HALF_Q, 128), CHAIN_LANES)
         gq[h] = dot(turned[...], dqkv[:, src], (1, 0)).astype(BF16)
-
-    def plane_terms(h):
-        src = pl.ds(pl.multiple_of(h * HALF_Q + CHAIN_LANES, 128), PLANE_LANES)
-        gp[h] = dot(turned_p[...], dqkv[:, src], (1, 0)).astype(BF16)
 
     def plane_sends(copy, keep):
         for d in range(1, 8):
@@ -417,12 +397,6 @@
     def keep_o(low):
         return pltpu.make_async_copy(
             stage_o.at[spot, :, 256 * low:256 * low + 384], final_o.at[half * 8], o_recv.at[half * 8]
-        )
-
-    def plane_p(d):
-        to = half * 8 + d
-        return remote(
-            stage_p.at[lax.rem(spot + d, 8)], final_p.at[to], op_send.at[d], op_recv.at[to], owner(d, 1)
         )
 
     late = m_all[2:4].reshape(HALF_ROWS, WIDTH)
@@ -469,12 +443,8 @@
                 chain_copy(way, k, n).start()
 
     chain_step(0)
-    turned_p[:, HALF_ROWS:] = dot(perm[...], late, (1, 1)).astype(BF16)
-    plane_terms(1 - core)
-    pair_copy_p().start()
     out_terms(1 - core)
     pair_copy_o().start()
-    plane_terms(core)
     out_terms(core)
     chain_step(1)
     pair_copy_o().wait_recv()
@@ -482,22 +452,6 @@
         at = slice(SLOT_E * j, SLOT_E * j + SLOT_E)
         stage_o[j] = (go[core, at, :].astype(F32) + xo[at, :].astype(F32)).astype(BF16)
     plane_sends(plane_o, keep_o)
-
-    pair_copy_p().wait_recv()
-    for j in range(8):
-        at = slice(BLOCK_Q * j, BLOCK_Q * j + BLOCK_Q)
-        stage_p[j] = (gp[core, at, :].astype(F32) + xp[at, :].astype(F32)).astype(BF16)
-    for d in range(1, 8):
-        plane_p(d).start()
-    own_p = jnp.logical_and(core == half, core == 1)
-
-    @pl.when(own_p)
-    def _():
-        pltpu.make_async_copy(stage_p.at[spot], final_p.at[half * 8], op_recv.at[half * 8]).start()
-
-    @pl.when(jnp.logical_not(own_p))
-    def _():
-        plane_p(0).start()
 
     gates = []
     for n in range(3):
@@ -574,20 +528,17 @@
     stage[...] = wide.reshape(8, 32, CHAIN_LANES)
 
     def from_stage(j, low):
-        return stage.at[j, :, 0:FINAL_LANES] if low == 0 else stage.at[j, :, 384:CHAIN_LANES]
-
-    def to_final(i, low):
-        return final.at[i] if low == 0 else final.at[i, :, 0:HIGH_LANES]
+        return stage.at[j, :, 384 * low:384 * low + FINAL_LANES]
 
     def plane_q(d, low):
         to = half * 8 + d
         return remote(
-            from_stage(lax.rem(spot + d, 8), low), to_final(to, low),
+            from_stage(lax.rem(spot + d, 8), low), final.at[to],
             f_send.at[d, low], f_recv.at[to], owner(d, low),
         )
 
     def keep_q(low):
-        return pltpu.make_async_copy(from_stage(spot, low), to_final(half * 8, low), f_recv.at[half * 8])
+        return pltpu.make_async_copy(from_stage(spot, low), final.at[half * 8], f_recv.at[half * 8])
 
     plane_sends(plane_q, keep_q)
 
@@ -620,17 +571,6 @@
     spread_o[...] = widen(plane_sum(final_o, o_recv).astype(BF16), 9, 16).reshape(8, 16, 384)
     for d in range(1, 8):
         last_copy(d).start()
-    def last_copy_p(d):
-        return remote(
-            spread_p.at[lax.rem(clip + d, 8)], last_p.at[d], lp_send.at[d], lp_recv.at[d], along(d)
-        )
-
-    @pl.when(core == 1)
-    def _():
-        spread_p[...] = widen(plane_sum(final_p, op_recv).astype(BF16), 18, 32).reshape(8, 32, PLANE_LANES)
-        for d in range(1, 8):
-            last_copy_p(d).start()
-
     total = spread_o[clip].astype(F32)
     for d in range(1, 8):
         last_copy(d).wait_recv()
@@ -645,33 +585,9 @@
     flats = [jnp.concatenate([mods[z, i:i + 1] for i in range(8)], 1) for z in range(8)]
     for i in range(3):
         d_mod[0, i] = jnp.concatenate([flat[:, WIDTH * i:WIDTH * i + WIDTH] for flat in flats], 0)
-    @pl.when(core == 0)
-    def _():
-        oq[...] = plane_sum(final, f_recv)[0:18, 0:SHARD_Q]
-
-    @pl.when(core == 1)
-    def _():
-        rest = spread_p[clip].astype(F32)
-        for d in range(1, 8):
-            last_copy_p(d).wait_recv()
-            rest = rest + last_p[d].astype(F32)
-        for i in range(16):
-            wait_bytes(to_final(i, 1), f_recv.at[i])
-        first = final[0, :, 0:HIGH_LANES].astype(F32)
-        for i in range(1, 16):
-            first = first + final[i, :, 0:HIGH_LANES].astype(F32)
-        oq[...] = jnp.concatenate([first[0:18, 48:HIGH_LANES], rest[0:18, 0:SHARD_Q - HIGH_FIRST]], 1)
-        for d in range(1, 8):
-            last_copy_p(d).wait_send()
-
-    for d in range(1, 8):
-        plane_p(d).wait_send()
-
-    @pl.when(jnp.logical_not(own_p))
-    def _():
-        plane_p(0).wait_send()
-
-    pair_copy_p().wait_send()
+    total = plane_sum(final, f_recv)
+    oq[...] = jnp.where(core == 0, total[:, 0:SHARD_Q], total[:, 48:48 + SHARD_Q])[0:18]
+
     plane_sent(plane_o)
     plane_sent(plane_q)
     for d in range(1, 8):
@@ -741,15 +657,13 @@
             held(2 * HALF_Q, WIDTH), held(WIDTH, HEADS * HD),
             held(ROWS, 2 * HALF_Q), held(ROWS, HEADS * HD), held(ROWS, HEADS * HD),
             held(ROWS, WIDTH), held(ROWS, 2 * HALF_Q),
-            held(WIDTH, ROWS), held(WIDTH, ROWS), held(WIDTH, WIDTH), held(CHUNKS, CHUNK, WIDTH),
-            held(2, WIDTH, CHAIN_LANES), held(2, WIDTH, PLANE_LANES), held(2, HEADS * SLOT_E, HALF_O),
+            held(WIDTH, ROWS), held(CHUNKS, CHUNK, WIDTH),
+            held(2, WIDTH, CHAIN_LANES), held(2, HEADS * SLOT_E, HALF_O),
             held(2, 8, 2, 16, WIDTH),
-            held(WIDTH, CHAIN_LANES), held(WIDTH, PLANE_LANES), held(HEADS * SLOT_E, HALF_O),
+            held(WIDTH, CHAIN_LANES), held(HEADS * SLOT_E, HALF_O),
             held(2, STEPS, BLOCK_Q, CHAIN_LANES), held(2, STEPS, BLOCK_Q, CHAIN_LANES),
             held(8, 32, CHAIN_LANES), held(16, 32, FINAL_LANES),
-            held(8, BLOCK_Q, PLANE_LANES), held(16, BLOCK_Q, PLANE_LANES),
-            held(8, 32, PLANE_LANES), held(8, 32, PLANE_LANES),
-            held(8, SLOT_E, HALF_O), held(16, SLOT_E, 384),
+                       held(8, SLOT_E, HALF_O), held(16, SLOT_E, 384),
             held(8, 16, 384), held(8, 16, 384),
             held(8, PACKED, dtype=F32), held(8, 8, PACKED, dtype=F32), held(8, 8, PACKED, dtype=F32),
             dma((5,)), dma((2, 2, 8)), dma((2, 2, 8)), dma((2,)), dma((2,)),
@@ -757,7 +671,6 @@
             dma((2, 8)), dma((2, 8)), dma((8,)), dma((8,)), dma(chains), dma(chains),
             dma((8,)), dma((8,)), dma((8,)), dma((8,)), dma((8, 2)), dma((16,)),
             dma, dma, dma((8, 2)), dma((16,)), dma((8,)), dma((8,)),
-            dma, dma, dma((8,)), dma((16,)), dma((8,)), dma((8,)),
         ],
         compiler_params=pltpu.CompilerParams(
             vmem_limit_bytes=VMEM_BYTES, collective_id=0, has_side_effects=True

time: 94.8 us -> 91.1 us (0.961)
  Pallas kernels: 93.8 us -> 90.1 us
    pallas_call x1, Pallas kernels: 91.5 us -> 87.7 us  [body(): pl.pallas_call(fused_kernel, out_shape=outs, in_specs=[anywhere, anywhere...]
where the time goes in v5:
time: 91.1 us; the launch traced here: 90.9 us
  Pallas kernels  90.1 us (99%)
    pallas_call x1, Pallas kernels, body(): pl.pallas_call(fused_kernel, out_shape=outs, in_specs=[anywhere, anywhere...  87.7 us
    pallas_call x1, Pallas kernels, body(): pl.pallas_call(copy_kernel, out_shape=outs, in_specs=[anywhere] * 4, out_...  2.37 us

profile of v5, /device:TPU:1, one launch (start us, length us, event | category | flops | bytes accessed | tf_op | source)
XLA Modules:
  0.0 90.9 jit_solution(8030454925082177793)
XLA Ops:
  0.6 87.7 %shard_map.84 = (bf16[1,2,256,1152]{3,2,1,0:T(8,128)(2,1)}, f32[1,3,8,1152]{3,2,1,0:T(8,128)}, f32[18,432]{1,0:T(8,128)}, f32[9,288]{1,0:T(8,128)}) custom-call(bf16[1,2,256,1152]{3,2,1,0:T(8,128)(2,1)} %tok_in.1, bf16[1,2,256,1152]{3,2,1,0:T(8,128)(2,1)} %dout_in.1, f32[1,3,8,1152]{3,2,1,0:T(8,128)} %bitcast.4, bf16[432,1152]{1,0:T(8,128)(2,1)} %wq.1, ...), custom_call_target="tpu_custom_call" | custom-call | tf_op jit(solution)/shard_map/pallas_call | solution.py:648
  88.4 2.4 %shard_map.85 = (bf16[1,2,256,1152]{3,2,1,0:T(8,128)(2,1)}, f32[1,3,8,1152]{3,2,1,0:T(8,128)}, f32[18,432]{1,0:T(8,128)}, f32[9,288]{1,0:T(8,128)}) custom-call(bf16[1,2,256,1152]{3,2,1,0:T(8,128)(2,1)} %get-tuple-element.12.refs_0_, f32[1,3,8,1152]{3,2,1,0:T(8,128)} %get-tuple-element.13.refs_1_, f32[18,432]{1,0:T(8,128)} %get-tuple-element.14.refs_2_, ...), custom_call_target="tpu_custom_call" | custom-call | tf_op jit(solution)/shard_map/pallas_call | solution.py:679
